TPU v7x, 32 devices: a whole 2x2x4 slice. The times are simulated.
32 devices in a mesh: dom: 32 (over z, y, x, core).
Axes of the slice: x: 2, y: 2, z: 4, core: 2. Of those that a mesh axis runs over, the one named last changes fastest.
Arguments:
- features: bfloat16 [16384, 256], P('dom'), may hold values from -20 to 20, as said below
- w_self: bfloat16 [256, 256], replicated, may hold values from -0.375 to 0.375
- w_neigh: bfloat16 [256, 256], replicated, may hold values from -0.375 to 0.375
- neighbors: int32 [16384, 10], P('dom'), may hold values from 0 to 1151
- degree: int32 [16384], P('dom'), may hold values from 1 to 10
- boundary: int32 [32, 5, 128], P('dom'), may hold values from 0 to 511
- upstream: bfloat16 [16384, 256], P('dom'), may hold values from -6 to 6
Outputs:
- hidden: bfloat16 [16384, 256], P('dom')
- node_grad: bfloat16 [16384, 256], P('dom')
- weight_step: float32 [512, 256], replicated
Inputs may be any that keep to these rules, and one draw needn't show every extreme that they name: `features`: feature values lie in the stated range.
All inputs are finite; a program needn't handle non-finite values.
Results may differ from a plain program's by a relative error of at most 0.006.
Values may be sent and summed in bfloat16 or wider, within the bound.
A program may use at most 64 MiB of HBM per device.

v0:
```python
import jax
import jax.numpy as jnp
from jax import lax
from jax.sharding import PartitionSpec as P

epsilon = 1e-06


def swapped(x, axis, apart):
    return lax.ppermute(x, axis, [(i, i ^ 1 << apart) for i in range(lax.axis_size(axis))])


def swap_rows(features, boundary_rows, levels):
    received = []
    for level in range(levels):
        received.append(swapped(features[boundary_rows[level]], "dom", level))
    return received


def scatter_slots(values, neighbors, degree, total_rows):
    table = jnp.zeros((total_rows, values.shape[1]), jnp.float32)
    for slot in range(neighbors.shape[1]):
        usable = (slot < degree)[:, None]
        table = table.at[neighbors[:, slot]].add(jnp.where(usable, values, jnp.float32(0.0)))
    return table


def per_device(features, w_self, w_neigh, neighbors, degree, boundary, upstream):
    levels = lax.axis_size("dom").bit_length() - 1
    node_dev = features.shape[0]
    feature_width = features.shape[1]
    slot_count = neighbors.shape[1]
    boundary_rows = boundary[0]
    bnd_rows = boundary_rows.shape[1]
    degree_float = degree.astype(jnp.float32)[:, None]
    extended = jnp.concatenate([features] + swap_rows(features, boundary_rows, levels), axis=0)
    summed = jnp.zeros((node_dev, feature_width), jnp.float32)
    for slot in range(slot_count):
        usable = (slot < degree)[:, None]
        summed = summed + jnp.where(
            usable, extended[neighbors[:, slot]].astype(jnp.float32), jnp.float32(0.0)
        )
    agg = (summed / degree_float).astype(jnp.bfloat16)
    pre_sum = jnp.dot(features, w_self, preferred_element_type=jnp.float32) + jnp.dot(
        agg, w_neigh, preferred_element_type=jnp.float32
    )
    hidden = jax.nn.silu(pre_sum).astype(jnp.bfloat16)
    sigmoid_pre = jax.nn.sigmoid(pre_sum)
    pre_grad = (
        upstream.astype(jnp.float32) * sigmoid_pre * (1.0 + pre_sum * (1.0 - sigmoid_pre))
    ).astype(jnp.bfloat16)
    row_contract = (((0,), (0,)), ((), ()))
    grad_self = lax.dot_general(
        features, pre_grad, row_contract, preferred_element_type=jnp.float32
    )
    grad_neigh = lax.dot_general(agg, pre_grad, row_contract, preferred_element_type=jnp.float32)
    stacked = jnp.concatenate([grad_self, grad_neigh], axis=0)
    total_grad = lax.psum(stacked, "dom")
    weight_step = total_grad * lax.rsqrt(jnp.mean(total_grad * total_grad) + epsilon)
    column_contract = (((1,), (1,)), ((), ()))
    self_grad = lax.dot_general(
        pre_grad, w_self, column_contract, preferred_element_type=jnp.float32
    )
    total_rows = node_dev + levels * bnd_rows
    slot_share = (
        lax.dot_general(pre_grad, w_neigh, column_contract, preferred_element_type=jnp.float32)
        / degree_float
    )
    ext_grad = scatter_slots(slot_share, neighbors, degree, total_rows)
    local_grad = self_grad + ext_grad[:node_dev]
    for level in range(levels):
        start_row = node_dev + level * bnd_rows
        returned = swapped(
            ext_grad[start_row : start_row + bnd_rows].astype(jnp.bfloat16), "dom", level
        ).astype(jnp.float32)
        local_grad = local_grad.at[boundary_rows[level]].add(returned)
    node_grad = local_grad.astype(jnp.bfloat16)
    return (hidden, node_grad, weight_step)


def solution(mesh):
    return jax.shard_map(
        per_device,
        mesh=mesh,
        in_specs=(
            P("dom", None),
            P(),
            P(),
            P("dom", None),
            P("dom"),
            P("dom", None, None),
            P("dom", None),
        ),
        out_specs=(P("dom", None), P("dom", None), P()),
        check_vma=False,
    )
```

profile of v0, /device:TPU:0, one launch (start us, length us, event | category | flops | bytes accessed | tf_op | source)
XLA Modules:
  0.0 229.3 jit_solution(11987025351104109190)
XLA Ops:
  12.1 2.6 %collective-permute-start.1 = (bf16[128,256]{1,0:T(8,128)(2,1)S(1)}, bf16[128,256]{1,0:T(8,128)(2,1)S(1)}, u32[]{:S(2)}, u32[]{:S(2)}) collective-permute-start(bf16[128,256]{1,0:T(8,128)(2,1)S(1)} %gather_fusion.1), channel_id=1, source_target_pairs={{0,2},{1,3},{2,0},{3,1},{4,6},{5,7},{6,4},{7,5},{8,10},{9,11},{10,... | collective-permute-start | bytes 196616 | tf_op jit(solution)/shard_map/ppermute | solution.py:10
  20.4 2.7 %collective-permute-start.4 = (bf16[128,256]{1,0:T(8,128)(2,1)S(1)}, bf16[128,256]{1,0:T(8,128)(2,1)S(1)}, u32[]{:S(2)}, u32[]{:S(2)}) collective-permute-start(bf16[128,256]{1,0:T(8,128)(2,1)S(1)} %gather_fusion.4), channel_id=1, source_target_pairs={{0,16},{1,17},{2,18},{3,19},{4,20},{5,21},{6,22},{7,23},{8,24},{9,... | collective-permute-start | bytes 196616 | tf_op jit(solution)/shard_map/ppermute | solution.py:10
  24.4 2.0 collective-permute-done.4
  26.4 2.1 gather_fusion.14
  28.5 2.0 gather_fusion.13
  30.4 2.0 gather_fusion.12
  32.4 2.0 gather_fusion.11
  34.4 2.0 gather_fusion.10
  36.3 2.0 gather_fusion.9
  38.3 2.0 gather_fusion.8
  44.2 2.6 %gather_fusion.5 = bf16[512,256]{1,0:T(8,128)(2,1)} fusion(bf16[1152,256]{1,0:T(8,128)(2,1)S(1)} %constant_dynamic-update-slice_fusion, s32[1024]{0:T(1024)S(1)} %get-tuple-element.44), kind=kCustom, calls=%fused_computation.5 | custom fusion | bytes 526336 | tf_op jit(solution)/shard_map/gather | solution.py:41
  46.8 2.6 %divide_convert_fusion = bf16[512,256]{1,0:T(8,128)(2,1)S(1)} fusion(bf16[512,256]{1,0:T(8,128)(2,1)S(1)} %gather_fusion.14, bf16[512,256]{1,0:T(8,128)(2,1)S(1)} %gather_fusion.13, bf16[512,256]{1,0:T(8,128)(2,1)S(1)} %gather_fusion.12, bf16[512,256]{1,0:T(8,128)(2,1)S(1)} %gather_fusion.11, bf16[512,256]{1,0:T(8,128)(2,1)S(1)} %gather_fusion.10, ...), kind=kLoop, calls=%fused_computation.60 | loop fusion | flops 4063232 | bytes 2890752 | tf_op jit(solution)/shard_map/convert_element_type | solution.py:43
  51.4 3.7 %scatter_custom_fusion = f32[1152,256]{1,0:T(8,128)S(1)} fusion(s32[512]{0:T(512)S(1)} %bitcast.63, f32[]{:T(128)} %constant.2.clone.1, f32[512,256]{1,0:T(8,128)S(1)} %convolution_divide_fusion, pred[512]{0:T(512)(128)(4,1)S(1)} %get-tuple-element.25), kind=kCustom, calls=%fused_computation.34 | custom fusion | flops 262144 | bytes 1705472 | tf_op jit(solution)/shard_map/scatter-add | solution.py:24
  55.1 4.3 %scatter_custom_fusion.1 = f32[1152,256]{1,0:T(8,128)S(1)} fusion(f32[1152,256]{1,0:T(8,128)S(1)} %scatter_custom_fusion, s32[512]{0:T(512)S(1)} %bitcast.61, f32[512,256]{1,0:T(8,128)S(1)} %convolution_divide_fusion, f32[]{:T(128)} %constant.2.clone.1, pred[512]{0:T(512)(128)(4,1)S(1)} %get-tuple-element.33), kind=kCustom, calls=%fused_computation.54 | custom fusion | flops 262144 | bytes 1704452 | tf_op jit(solution)/shard_map/scatter-add | solution.py:24
  59.4 3.9 %scatter_custom_fusion.2 = f32[1152,256]{1,0:T(8,128)S(1)} fusion(f32[1152,256]{1,0:T(8,128)S(1)} %scatter_custom_fusion.1, s32[512]{0:T(512)S(1)} %bitcast.59, f32[512,256]{1,0:T(8,128)S(1)} %convolution_divide_fusion, f32[]{:T(128)} %constant.2.clone.1, pred[512]{0:T(512)(128)(4,1)S(1)} %get-tuple-element.32), kind=kCustom, calls=%fused_computation.52 | custom fusion | flops 262144 | bytes 1704452 | tf_op jit(solution)/shard_map/scatter-add | solution.py:24
  63.4 3.9 %scatter_custom_fusion.3 = f32[1152,256]{1,0:T(8,128)S(1)} fusion(f32[1152,256]{1,0:T(8,128)S(1)} %scatter_custom_fusion.2, s32[512]{0:T(512)S(1)} %bitcast.57, f32[512,256]{1,0:T(8,128)S(1)} %convolution_divide_fusion, f32[]{:T(128)} %constant.2.clone.1, pred[512]{0:T(512)(128)(4,1)S(1)} %get-tuple-element.31), kind=kCustom, calls=%fused_computation.50 | custom fusion | flops 262144 | bytes 1704452 | tf_op jit(solution)/shard_map/scatter-add | solution.py:24
  67.3 3.9 %scatter_custom_fusion.4 = f32[1152,256]{1,0:T(8,128)S(1)} fusion(f32[1152,256]{1,0:T(8,128)S(1)} %scatter_custom_fusion.3, s32[512]{0:T(512)S(1)} %bitcast.55, f32[512,256]{1,0:T(8,128)S(1)} %convolution_divide_fusion, f32[]{:T(128)} %constant.2.clone.1, pred[512]{0:T(512)(128)(4,1)S(1)} %get-tuple-element.30), kind=kCustom, calls=%fused_computation.48 | custom fusion | flops 262144 | bytes 1704452 | tf_op jit(solution)/shard_map/scatter-add | solution.py:24
  71.2 3.9 %scatter_custom_fusion.5 = f32[1152,256]{1,0:T(8,128)S(1)} fusion(f32[1152,256]{1,0:T(8,128)S(1)} %scatter_custom_fusion.4, s32[512]{0:T(512)S(1)} %bitcast.53, f32[512,256]{1,0:T(8,128)S(1)} %convolution_divide_fusion, f32[]{:T(128)} %constant.2.clone.1, pred[512]{0:T(512)(128)(4,1)S(1)} %get-tuple-element.29), kind=kCustom, calls=%fused_computation.46 | custom fusion | flops 262144 | bytes 1704452 | tf_op jit(solution)/shard_map/scatter-add | solution.py:24
  75.1 4.1 %scatter_custom_fusion.6 = f32[1152,256]{1,0:T(8,128)S(1)} fusion(f32[1152,256]{1,0:T(8,128)S(1)} %scatter_custom_fusion.5, s32[512]{0:T(512)S(1)} %bitcast.51, f32[512,256]{1,0:T(8,128)S(1)} %convolution_divide_fusion, f32[]{:T(128)} %constant.2.clone.1, pred[512]{0:T(512)(128)(4,1)S(1)} %get-tuple-element.28), kind=kCustom, calls=%fused_computation.44 | custom fusion | flops 262144 | bytes 1704452 | tf_op jit(solution)/shard_map/scatter-add | solution.py:24
  79.2 3.9 %scatter_custom_fusion.7 = f32[1152,256]{1,0:T(8,128)S(1)} fusion(f32[1152,256]{1,0:T(8,128)S(1)} %scatter_custom_fusion.6, s32[512]{0:T(512)S(1)} %bitcast.49, f32[512,256]{1,0:T(8,128)S(1)} %convolution_divide_fusion, f32[]{:T(128)} %constant.2.clone.1, pred[512]{0:T(512)(128)(4,1)S(1)} %get-tuple-element.27), kind=kCustom, calls=%fused_computation.42 | custom fusion | flops 262144 | bytes 1704452 | tf_op jit(solution)/shard_map/scatter-add | solution.py:24
  83.1 3.9 %scatter_custom_fusion.8 = f32[1152,256]{1,0:T(8,128)S(1)} fusion(f32[1152,256]{1,0:T(8,128)S(1)} %scatter_custom_fusion.7, s32[512]{0:T(512)S(1)} %bitcast.47, f32[512,256]{1,0:T(8,128)S(1)} %convolution_divide_fusion, f32[]{:T(128)} %constant.2.clone.1, pred[512]{0:T(512)(128)(4,1)S(1)} %get-tuple-element.26), kind=kCustom, calls=%fused_computation.40 | custom fusion | flops 262144 | bytes 1704452 | tf_op jit(solution)/shard_map/scatter-add | solution.py:24
  87.0 3.9 %scatter_custom_fusion.9 = f32[1152,256]{1,0:T(8,128)S(1)} fusion(f32[1152,256]{1,0:T(8,128)S(1)} %scatter_custom_fusion.8, s32[512]{0:T(512)S(1)} %bitcast.45, f32[512,256]{1,0:T(8,128)S(1)} %convolution_divide_fusion, f32[]{:T(128)} %constant.2.clone.1, pred[512]{0:T(512)(128)(4,1)S(1)} %get-tuple-element.34), kind=kCustom, calls=%fused_computation.38 | custom fusion | flops 262144 | bytes 1704452 | tf_op jit(solution)/shard_map/scatter-add | solution.py:24
  93.0 2.8 %collective-permute-start.9 = (bf16[128,256]{1,0:T(8,128)(2,1)S(1)}, bf16[128,256]{1,0:T(8,128)(2,1)S(1)}, u32[]{:S(2)}, u32[]{:S(2)}) collective-permute-start(bf16[128,256]{1,0:T(8,128)(2,1)S(1)} %get-tuple-element.3), channel_id=1, source_target_pairs={{0,16},{1,17},{2,18},{3,19},{4,20},{5,21},{6,22},{7,23},{8,24},{9,... | collective-permute-start | bytes 196616 | tf_op jit(solution)/shard_map/ppermute | solution.py:10
  104.5 113.4 %all-reduce.2.cloned.1.call-done = f32[512,256]{1,0:T(8,128)} async-done(((f32[512,256]{1,0:T(8,128)}), f32[512,256]{1,0:T(8,128)}) %all-reduce.2.cloned.1.call-update) | async-done | bytes 524304 | tf_op jit(solution)/shard_map/psum | solution.py:58
  (80 shorter events, 32.0 us)
Async XLA Ops:
  7.2 42.2 %copy-start = (bf16[256,256]{1,0:T(8,128)(2,1)S(1)}, bf16[256,256]{1,0:T(8,128)(2,1)}, u32[]{:S(2)}) copy-start(bf16[256,256]{1,0:T(8,128)(2,1)} %param.9) | copy-start | bytes 393220
  7.2 7.5 %copy-start.1 = (bf16[512,256]{1,0:T(8,128)(2,1)S(1)}, bf16[512,256]{1,0:T(8,128)(2,1)}, u32[]{:S(2)}) copy-start(bf16[512,256]{1,0:T(8,128)(2,1)} %param.7) | copy-start | bytes 786436
  7.2 210.7 %all-reduce.2.cloned.1.call-start = ((), (), s32[]{:S(2)}) async-start(), calls=%async_computation | async-start | bytes 1048576 | tf_op jit(solution)/shard_map/psum | solution.py:58
  8.0 9.9 %copy-start.7 = (s32[128]{0:T(128)}, s32[128]{0:T(128)S(1)}, u32[]{:S(2)}) copy-start(s32[128]{0:T(128)S(1)} %get-tuple-element.23) | copy-start | bytes 1540
  9.8 14.5 %collective-permute-start = (bf16[128,256]{1,0:T(8,128)(2,1)S(1)}, bf16[128,256]{1,0:T(8,128)(2,1)S(1)}, u32[]{:S(2)}, u32[]{:S(2)}) collective-permute-start(bf16[128,256]{1,0:T(8,128)(2,1)S(1)} %gather_fusion), channel_id=1, source_target_pairs={{0,1},{1,0},{2,3},{3,2},{4,5},{5,4},{6,7},{7,6},{8,9},{9,8},{10,11... | collective-permute-start | bytes 196616 | tf_op jit(solution)/shard_map/ppermute | solution.py:10
  12.0 11.1 %copy-start.6 = (s32[512]{0:T(512)S(1)}, s32[512]{0:T(512)}, u32[]{:S(2)}) copy-start(s32[512]{0:T(512)} %param.11) | copy-start | bytes 6148
  12.1 11.1 %copy-start.3 = (bf16[256,256]{1,0:T(8,128)(2,1)S(1)}, bf16[256,256]{1,0:T(8,128)(2,1)}, u32[]{:S(2)}) copy-start(bf16[256,256]{1,0:T(8,128)(2,1)} %param.8) | copy-start | bytes 393220
  12.1 12.3 %collective-permute-start.1 = (bf16[128,256]{1,0:T(8,128)(2,1)S(1)}, bf16[128,256]{1,0:T(8,128)(2,1)S(1)}, u32[]{:S(2)}, u32[]{:S(2)}) collective-permute-start(bf16[128,256]{1,0:T(8,128)(2,1)S(1)} %gather_fusion.1), channel_id=1, source_target_pairs={{0,2},{1,3},{2,0},{3,1},{4,6},{5,7},{6,4},{7,5},{8,10},{9,11},{10,... | collective-permute-start | bytes 196616 | tf_op jit(solution)/shard_map/ppermute | solution.py:10
  15.5 8.9 %collective-permute-start.2 = (bf16[128,256]{1,0:T(8,128)(2,1)S(1)}, bf16[128,256]{1,0:T(8,128)(2,1)S(1)}, u32[]{:S(2)}, u32[]{:S(2)}) collective-permute-start(bf16[128,256]{1,0:T(8,128)(2,1)S(1)} %gather_fusion.2), channel_id=1, source_target_pairs={{0,4},{1,5},{2,6},{3,7},{4,0},{5,1},{6,2},{7,3},{8,12},{9,13},{10,... | collective-permute-start | bytes 196616 | tf_op jit(solution)/shard_map/ppermute | solution.py:10
  17.1 7.1 %copy-start.5 = (s32[512,10]{0,1:T(8,128)S(1)}, s32[512,10]{0,1:T(8,128)}, u32[]{:S(2)}) copy-start(s32[512,10]{0,1:T(8,128)} %param.10) | copy-start | bytes 61444
  18.0 6.4 %collective-permute-start.3 = (bf16[128,256]{1,0:T(8,128)(2,1)S(1)}, bf16[128,256]{1,0:T(8,128)(2,1)S(1)}, u32[]{:S(2)}, u32[]{:S(2)}) collective-permute-start(bf16[128,256]{1,0:T(8,128)(2,1)S(1)} %gather_fusion.3), channel_id=1, source_target_pairs={{0,8},{1,9},{2,10},{3,11},{4,12},{5,13},{6,14},{7,15},{8,0},{9,1},... | collective-permute-start | bytes 196616 | tf_op jit(solution)/shard_map/ppermute | solution.py:10
  20.4 5.9 %collective-permute-start.4 = (bf16[128,256]{1,0:T(8,128)(2,1)S(1)}, bf16[128,256]{1,0:T(8,128)(2,1)S(1)}, u32[]{:S(2)}, u32[]{:S(2)}) collective-permute-start(bf16[128,256]{1,0:T(8,128)(2,1)S(1)} %gather_fusion.4), channel_id=1, source_target_pairs={{0,16},{1,17},{2,18},{3,19},{4,20},{5,21},{6,22},{7,23},{8,24},{9,... | collective-permute-start | bytes 196616 | tf_op jit(solution)/shard_map/ppermute | solution.py:10
  46.8 2.7 %copy-start.2 = (f32[512,256]{1,0:T(8,128)S(1)}, f32[512,256]{1,0:T(8,128)}, u32[]{:S(2)}) copy-start(f32[512,256]{1,0:T(8,128)} %fusion.57) | copy-start | bytes 1572868
  46.8 2.7 %copy-start.8 = (bf16[512,256]{1,0:T(8,128)(2,1)S(1)}, bf16[512,256]{1,0:T(8,128)(2,1)}, u32[]{:S(2)}) copy-start(bf16[512,256]{1,0:T(8,128)(2,1)} %param.13) | copy-start | bytes 786436
  91.0 4.8 %copy-start.4 = (bf16[256,256]{1,0:T(8,128)(2,1)S(1)}, bf16[256,256]{1,0:T(8,128)(2,1)}, u32[]{:S(2)}) copy-start(bf16[256,256]{1,0:T(8,128)(2,1)} %param.8) | copy-start | bytes 393220
  91.9 4.2 %collective-permute-start.5 = (bf16[128,256]{1,0:T(8,128)(2,1)S(1)}, bf16[128,256]{1,0:T(8,128)(2,1)S(1)}, u32[]{:S(2)}, u32[]{:S(2)}) collective-permute-start(bf16[128,256]{1,0:T(8,128)(2,1)S(1)} %get-tuple-element.7), channel_id=1, source_target_pairs={{0,1},{1,0},{2,3},{3,2},{4,5},{5,4},{6,7},{7,6},{8,9},{9,8},{10,11... | collective-permute-start | bytes 196616 | tf_op jit(solution)/shard_map/ppermute | solution.py:10
  92.0 5.8 %collective-permute-start.6 = (bf16[128,256]{1,0:T(8,128)(2,1)S(1)}, bf16[128,256]{1,0:T(8,128)(2,1)S(1)}, u32[]{:S(2)}, u32[]{:S(2)}) collective-permute-start(bf16[128,256]{1,0:T(8,128)(2,1)S(1)} %get-tuple-element.6), channel_id=1, source_target_pairs={{0,2},{1,3},{2,0},{3,1},{4,6},{5,7},{6,4},{7,5},{8,10},{9,11},{10,... | collective-permute-start | bytes 196616 | tf_op jit(solution)/shard_map/ppermute | solution.py:10
  92.6 6.7 %collective-permute-start.7 = (bf16[128,256]{1,0:T(8,128)(2,1)S(1)}, bf16[128,256]{1,0:T(8,128)(2,1)S(1)}, u32[]{:S(2)}, u32[]{:S(2)}) collective-permute-start(bf16[128,256]{1,0:T(8,128)(2,1)S(1)} %get-tuple-element.5), channel_id=1, source_target_pairs={{0,4},{1,5},{2,6},{3,7},{4,0},{5,1},{6,2},{7,3},{8,12},{9,13},{10,... | collective-permute-start | bytes 196616 | tf_op jit(solution)/shard_map/ppermute | solution.py:10
  93.0 7.8 %collective-permute-start.8 = (bf16[128,256]{1,0:T(8,128)(2,1)S(1)}, bf16[128,256]{1,0:T(8,128)(2,1)S(1)}, u32[]{:S(2)}, u32[]{:S(2)}) collective-permute-start(bf16[128,256]{1,0:T(8,128)(2,1)S(1)} %get-tuple-element.4), channel_id=1, source_target_pairs={{0,8},{1,9},{2,10},{3,11},{4,12},{5,13},{6,14},{7,15},{8,0},{9,1},... | collective-permute-start | bytes 196616 | tf_op jit(solution)/shard_map/ppermute | solution.py:10
  93.0 9.3 %collective-permute-start.9 = (bf16[128,256]{1,0:T(8,128)(2,1)S(1)}, bf16[128,256]{1,0:T(8,128)(2,1)S(1)}, u32[]{:S(2)}, u32[]{:S(2)}) collective-permute-start(bf16[128,256]{1,0:T(8,128)(2,1)S(1)} %get-tuple-element.3), channel_id=1, source_target_pairs={{0,16},{1,17},{2,18},{3,19},{4,20},{5,21},{6,22},{7,23},{8,24},{9,... | collective-permute-start | bytes 196616 | tf_op jit(solution)/shard_map/ppermute | solution.py:10
Sparse Core Ops, SparseCore 0:
  92.0 125.9 all-reduce.1
where the time goes:
time: 232 us; the launch traced here: 229 us
  waiting for transfers between devices  115 us (50%)
  other arithmetic  55.9 us (24%)
  local copies, waits for them, and re-layouts  26.5 us (11%)
  between operations  15.4 us (7%)
  starting transfers between devices  12.9 us (6%)
  matrix products  3.21 us (1%)
    psum x1, waiting for transfers between devices, per_device(): total_grad = lax.psum(stacked, 'dom')  113 us
    scatter-add x10, other arithmetic, scatter_slots(): table.at[neighbors[:, slot]]  39.4 us
    gather x10, local copies, waits for them, and re-layouts, per_device(): extended[neighbors[:, slot]].astype(jnp.float32)  20.3 us
    ppermute x10, starting transfers between devices, swapped(): lax.ppermute(x, axis, [(i, i ^ 1 << apart) for i in range(lax.axis_size(a...  12.9 us
    scatter-add x5, other arithmetic, per_device(): local_grad = local_grad.at[boundary_rows[level]].add(returned)  7.63 us
    gather x5, local copies, waits for them, and re-layouts, swap_rows(): received.append(swapped(features[boundary_rows[level]], 'dom', level))  6.02 us
  transfers between devices with their start and end apart: 11, of which 2 were waited for; matrix products, arithmetic and copies ran while one was open for 6% of the time, Pallas kernels for 0%

commit v1 on v0

v1 whole, which is shorter than its diff:
```python
import functools

import jax
import jax.numpy as jnp
from jax import lax
from jax.experimental import pallas as pl
from jax.experimental.pallas import tpu as pltpu
from jax.sharding import PartitionSpec as P

epsilon = 1e-06
INNER_BITS = 3
BUILD_ROWS = 64


def partner(me, mask):
    other = me
    bit = 0
    while mask >> bit:
        if (mask >> bit) & 1:
            size = 1 << bit
            other = other + size * (1 - 2 * lax.rem(lax.div(me, size), 2))
        bit += 1
    return other


def dot(a, b):
    return jnp.dot(a, b, preferred_element_type=jnp.float32)


def dot_rows(a, b):
    return lax.dot_general(a, b, (((0,), (0,)), ((), ())), preferred_element_type=jnp.float32)


def dot_cols(a, b):
    return lax.dot_general(a, b, (((1,), (1,)), ((), ())), preferred_element_type=jnp.float32)


def kernel(
    inner, outer, levels, bnd,
    feat_ref, w_self_ref, w_neigh_ref, slots_ref, degree_ref, boundary_ref, up_ref,
    hidden_ref, node_ref, step_ref,
    table, pick, out_rows, in_rows, out_grads, in_grads,
    stack, part_in, part, plane_in, gathered,
    row_ss, row_rs, grad_ss, grad_rs, part_ss, part_rs, plane_ss, plane_rs, gather_ss, gather_rs,
):
    me = lax.axis_index("dom")
    nodes = feat_ref.shape[0]
    slot_count = slots_ref.shape[0]
    total_rows = table.shape[0]
    chunk = stack.shape[0] // inner
    mine = lax.rem(me, inner)

    inner_masks = list(range(1, inner))
    outer_masks = [e * inner for e in range(1, outer)]
    barrier = pltpu.get_barrier_semaphore()
    for mask in inner_masks + outer_masks:
        pl.semaphore_signal(
            barrier, inc=1, device_id=(partner(me, mask),), device_id_type=pl.DeviceIdType.MESH
        )

    def remote(src, dst, send_sem, recv_sem, mask):
        return pltpu.make_async_remote_copy(
            src_ref=src, dst_ref=dst, send_sem=send_sem, recv_sem=recv_sem,
            device_id=(partner(me, mask),), device_id_type=pl.DeviceIdType.MESH,
        )

    feat = feat_ref[...]

    row_id = lax.broadcasted_iota(jnp.int32, (nodes, bnd), 0)
    row_copies = [None] * levels
    for place, level in enumerate(reversed(range(levels))):
        hot = (row_id == boundary_ref[level]).astype(jnp.float32).astype(jnp.bfloat16)
        span = pl.ds(level * bnd, bnd)
        pick[:, span] = hot
        out_rows[span, :] = dot_rows(hot, feat).astype(jnp.bfloat16)
        if place == 0:
            pl.semaphore_wait(barrier, len(inner_masks) + len(outer_masks))
        row_copies[level] = remote(
            out_rows.at[span, :], in_rows.at[span, :], row_ss.at[level], row_rs.at[level], 1 << level
        )
        row_copies[level].start()

    degree_row = degree_ref[...].reshape(1, nodes)
    named = [
        jnp.where(degree_row > slot, slots_ref[slot : slot + 1, :], -1) for slot in range(slot_count)
    ]

    def build(block, carry):
        start = pl.multiple_of(block * BUILD_ROWS, BUILD_ROWS)
        row = lax.broadcasted_iota(jnp.int32, (BUILD_ROWS, nodes), 0) + start
        count = jnp.zeros((BUILD_ROWS, nodes), jnp.float32)
        for slot in range(slot_count):
            count = jnp.where(row == named[slot], count + 1.0, count)
        table[pl.ds(start, BUILD_ROWS), :] = count.astype(jnp.bfloat16)
        return carry

    lax.fori_loop(0, total_rows // BUILD_ROWS, build, 0)

    share_row = 1.0 / degree_row.astype(jnp.float32)
    share = jnp.transpose(jnp.broadcast_to(share_row, (128, nodes)))
    share = jnp.concatenate([share] * (feat.shape[1] // 128), axis=1)

    summed = dot_rows(table[:nodes, :], feat)
    pre_self = dot(feat, w_self_ref[...])
    for level in range(levels):
        row_copies[level].wait_recv()
    summed = summed + dot_rows(table[nodes:, :], in_rows[...])
    agg = (summed * share).astype(jnp.bfloat16)
    pre_sum = pre_self + dot(agg, w_neigh_ref[...])
    sigmoid = jax.nn.sigmoid(pre_sum)
    hidden_ref[...] = (pre_sum * sigmoid).astype(jnp.bfloat16)
    pre_grad = (
        up_ref[...].astype(jnp.float32) * sigmoid * (1.0 + pre_sum * (1.0 - sigmoid))
    ).astype(jnp.bfloat16)

    width = feat.shape[1]
    stack[:width, :] = dot_rows(feat, pre_grad).astype(jnp.bfloat16)
    stack[width:, :] = dot_rows(agg, pre_grad).astype(jnp.bfloat16)
    part_copies = []
    for mask in inner_masks:
        theirs = lax.rem(partner(me, mask), inner)
        copy = remote(
            stack.at[pl.ds(pl.multiple_of(theirs * chunk, chunk), chunk), :],
            part_in.at[mask], part_ss.at[mask], part_rs.at[mask], mask,
        )
        copy.start()
        part_copies.append(copy)

    slot_share = (dot_cols(pre_grad, w_neigh_ref[...]) * share).astype(jnp.bfloat16)
    out_grads[...] = dot(table[nodes:, :], slot_share).astype(jnp.bfloat16)
    grad_copies = []
    for level in reversed(range(levels)):
        span = pl.ds(level * bnd, bnd)
        copy = remote(
            out_grads.at[span, :], in_grads.at[span, :], grad_ss.at[level], grad_rs.at[level], 1 << level
        )
        copy.start()
        grad_copies.append(copy)
    local = dot_cols(pre_grad, w_self_ref[...]) + dot(table[:nodes, :], slot_share)

    own = pl.ds(pl.multiple_of(mine * chunk, chunk), chunk)
    for copy in part_copies:
        copy.wait_recv()
    total = stack[own, :].astype(jnp.float32)
    for mask in inner_masks:
        total = total + part_in[mask].astype(jnp.float32)
    part[...] = total.astype(jnp.bfloat16)
    plane_copies = []
    for index, mask in enumerate(outer_masks):
        copy = remote(part, plane_in.at[index + 1], plane_ss.at[index + 1], plane_rs.at[index + 1], mask)
        copy.start()
        plane_copies.append(copy)

    for copy in grad_copies:
        copy.wait_recv()
    node_ref[...] = (local + dot(pick[...], in_grads[...])).astype(jnp.bfloat16)

    for copy in plane_copies:
        copy.wait_recv()
    terms = [part[...].astype(jnp.float32)]
    for index in range(1, outer):
        terms.append(plane_in[index].astype(jnp.float32))
    while len(terms) > 1:
        terms = [terms[i] + terms[i + 1] for i in range(0, len(terms), 2)]
    gathered[own, :] = terms[0].astype(jnp.bfloat16)
    gather_copies = []
    for mask in inner_masks:
        copy = remote(
            gathered.at[own, :], gathered.at[own, :], gather_ss.at[mask], gather_rs.at[mask], mask
        )
        copy.start()
        gather_copies.append(copy)
    for copy in gather_copies:
        copy.wait_recv()
    whole = gathered[...].astype(jnp.float32)
    step_ref[...] = whole * lax.rsqrt(jnp.mean(whole * whole) + epsilon)

    for copy in row_copies + part_copies + grad_copies + plane_copies + gather_copies:
        copy.wait_send()


def per_device(features, w_self, w_neigh, neighbors, degree, boundary, upstream):
    size = lax.axis_size("dom")
    levels = size.bit_length() - 1
    inner = min(size, 1 << INNER_BITS)
    outer = size // inner
    nodes, width = features.shape
    bnd = boundary.shape[2]
    rows = levels * bnd
    chunk = 2 * width // inner
    bf16 = jnp.bfloat16
    sem = pltpu.SemaphoreType.DMA
    vmem = pl.BlockSpec(memory_space=pltpu.VMEM)
    return pl.pallas_call(
        functools.partial(kernel, inner, outer, levels, bnd),
        out_shape=(
            jax.ShapeDtypeStruct((nodes, width), bf16),
            jax.ShapeDtypeStruct((nodes, width), bf16),
            jax.ShapeDtypeStruct((2 * width, width), jnp.float32),
        ),
        in_specs=[vmem] * 7,
        out_specs=(vmem, vmem, vmem),
        scratch_shapes=[
            pltpu.VMEM((nodes + rows, nodes), bf16),
            pltpu.VMEM((nodes, rows), bf16),
            pltpu.VMEM((rows, width), bf16),
            pltpu.VMEM((rows, width), bf16),
            pltpu.VMEM((rows, width), bf16),
            pltpu.VMEM((rows, width), bf16),
            pltpu.VMEM((2 * width, width), bf16),
            pltpu.VMEM((inner, chunk, width), bf16),
            pltpu.VMEM((chunk, width), bf16),
            pltpu.VMEM((outer, chunk, width), bf16),
            pltpu.VMEM((2 * width, width), bf16),
            sem((levels,)), sem((levels,)), sem((levels,)), sem((levels,)),
            sem((inner,)), sem((inner,)), sem((outer,)), sem((outer,)), sem((inner,)), sem((inner,)),
        ],
        compiler_params=pltpu.CompilerParams(
            collective_id=0, has_side_effects=True, vmem_limit_bytes=40 << 20
        ),
        cost_estimate=pl.CostEstimate(flops=1 << 30, bytes_accessed=3 << 20, transcendentals=nodes * width),
    )(features, w_self, w_neigh, neighbors.T, degree, boundary.transpose(1, 0, 2), upstream)


def solution(mesh):
    return jax.shard_map(
        per_device,
        mesh=mesh,
        in_specs=(
            P("dom", None),
            P(),
            P(),
            P("dom", None),
            P("dom"),
            P("dom", None, None),
            P("dom", None),
        ),
        out_specs=(P("dom", None), P("dom", None), P()),
        check_vma=False,
    )
```

time: 232 us -> 36.2 us (0.16); the launches traced: 229 us -> 35.8 us
  waiting for transfers between devices: 115 us -> 0 us
  other arithmetic: 55.9 us -> 0 us
  Pallas kernels: 0 us -> 27.2 us
  local copies, waits for them, and re-layouts: 26.5 us -> 8.02 us
  between operations: 15.4 us -> 0.66 us
  starting transfers between devices: 12.9 us -> 0 us
  matrix products: 3.21 us -> 0 us
    psum x1 -> x0, waiting for transfers between devices: 113 us -> none  [per_device(): total_grad = lax.psum(stacked, 'dom')]
    scatter-add x15 -> x0, other arithmetic: 47.1 us -> none  [the longest x10 39.4 us: scatter_slots(): table.at[neighbors[:, slot]]]
    pallas_call x0 -> x1, Pallas kernels: none -> 27.2 us  [per_device(): pl.pallas_call(functools.partial(kernel, inner, outer, levels, bnd), out_...]
    gather x15 -> x0, local copies, waits for them, and re-layouts: 26.3 us -> none  [the longest x10 20.3 us: per_device(): extended[neighbors[:, slot]].astype(jnp.float32)]
    ppermute x10 -> x0, starting transfers between devices: 12.9 us -> none  [swapped(): lax.ppermute(x, axis, [(i, i ^ 1 << apart) for i in range(lax.axis_size(a...]
    unnamed x23 -> x17, local copies, waits for them, and re-layouts: 0.09 us -> 8.02 us
    convert_element_type x3 -> x0, other arithmetic: 3.37 us -> none  [the longest x1 2.64 us: per_device(): agg = (summed / degree_float).astype(jnp.bfloat16)]
    dot_general x6 -> x0, matrix products: 3.21 us -> none  [the longest x1 1.13 us: per_device(): jnp.dot(agg, w_neigh, preferred_element_type=jnp.float32)]
  transfers between devices with their start and end apart: 11 -> 0, of which waited for: 2 -> 0; matrix products, arithmetic and copies ran while one was open for 6% -> 0% of each run, Pallas kernels for 0% -> 0%
where the time goes in v1:
time: 36.2 us; the launch traced here: 35.8 us
  Pallas kernels  27.2 us (75%)
  local copies, waits for them, and re-layouts  8.02 us (22%)
  between operations  0.66 us (2%)
    pallas_call x1, Pallas kernels, per_device(): pl.pallas_call(functools.partial(kernel, inner, outer, levels, bnd), out_...  27.2 us
    unnamed x17, local copies, waits for them, and re-layouts  8.02 us

profile of v1, /device:TPU:0, one launch (start us, length us, event | category | flops | bytes accessed | tf_op | source)
XLA Modules:
  0.0 35.8 jit_solution(5680809597302269132)
XLA Ops:
  0.6 0.0 copy-start.5
  0.6 0.7 %copy-done.5 = s32[1,5,128]{2,0,1:T(1,128)S(1)} copy-done((s32[1,5,128]{2,0,1:T(1,128)S(1)}, s32[1,5,128]{2,0,1:T(1,128)}, u32[]{:S(2)}) %copy-start.5) | copy-done | bytes 2584
  1.3 0.0 copy-start
  1.3 0.9 %copy-done = bf16[512,256]{1,0:T(8,128)(2,1)S(1)} copy-done((bf16[512,256]{1,0:T(8,128)(2,1)S(1)}, bf16[512,256]{1,0:T(8,128)(2,1)}, u32[]{:S(2)}) %copy-start) | copy-done | bytes 262168
  2.3 0.0 copy-start.1
  2.3 0.9 %copy-done.1 = bf16[512,256]{1,0:T(8,128)(2,1)S(1)} copy-done((bf16[512,256]{1,0:T(8,128)(2,1)S(1)}, bf16[512,256]{1,0:T(8,128)(2,1)}, u32[]{:S(2)}) %copy-start.1) | copy-done | bytes 262168
  3.2 0.0 copy-start.2
  3.2 0.9 %copy-done.2 = bf16[256,256]{1,0:T(8,128)(2,1)S(1)} copy-done((bf16[256,256]{1,0:T(8,128)(2,1)S(1)}, bf16[256,256]{1,0:T(8,128)(2,1)}, u32[]{:S(2)}) %copy-start.2) | copy-done | bytes 131096
  4.1 0.0 copy-start.3
  4.1 0.9 %copy-done.3 = bf16[256,256]{1,0:T(8,128)(2,1)S(1)} copy-done((bf16[256,256]{1,0:T(8,128)(2,1)S(1)}, bf16[256,256]{1,0:T(8,128)(2,1)}, u32[]{:S(2)}) %copy-start.3) | copy-done | bytes 131096
  5.0 0.0 copy-start.4
  5.0 0.8 %copy-done.4 = s32[512,10]{0,1:T(8,128)S(1)} copy-done((s32[512,10]{0,1:T(8,128)S(1)}, s32[512,10]{0,1:T(8,128)}, u32[]{:S(2)}) %copy-start.4) | copy-done | bytes 20504
  5.8 0.0 copy-start.6
  5.8 0.7 %copy-done.6 = s32[512]{0:T(512)S(1)} copy-done((s32[512]{0:T(512)S(1)}, s32[512]{0:T(512)}, u32[]{:S(2)}) %copy-start.6) | copy-done | bytes 2072
  6.5 27.2 %shard_map.94 = (bf16[512,256]{1,0:T(8,128)(2,1)S(1)}, bf16[512,256]{1,0:T(8,128)(2,1)S(1)}, f32[512,256]{1,0:T(8,128)S(1)}) custom-call(bf16[512,256]{1,0:T(8,128)(2,1)S(1)} %copy-done, bf16[256,256]{1,0:T(8,128)(2,1)S(1)} %copy-done.2, bf16[256,256]{1,0:T(8,128)(2,1)S(1)} %copy-done.3, s32[10,512]{1,0:T(8,128)S(1)} %bitcast.2, s32[512]{0:T(512)S(1)} %copy-done.6, ...), custom_call_target="tpu_custom_call" | custom-call | flops 1073741824 | bytes 3145728 | tf_op jit(solution)/shard_map/pallas_call | solution.py:194
  33.6 0.7 %copy.13 = bf16[512,256]{1,0:T(8,128)(2,1)} copy(bf16[512,256]{1,0:T(8,128)(2,1)S(1)} %get-tuple-element.6) | data formatting | bytes 524288
  34.3 0.7 %copy.14 = bf16[512,256]{1,0:T(8,128)(2,1)} copy(bf16[512,256]{1,0:T(8,128)(2,1)S(1)} %get-tuple-element.7) | data formatting | bytes 524288
  35.0 0.8 %copy.15 = f32[512,256]{1,0:T(8,128)} copy(f32[512,256]{1,0:T(8,128)S(1)} %get-tuple-element.8) | data formatting | bytes 1048576
Async XLA Ops:
  0.6 0.7 %copy-start.5 = (s32[1,5,128]{2,0,1:T(1,128)S(1)}, s32[1,5,128]{2,0,1:T(1,128)}, u32[]{:S(2)}) copy-start(s32[1,5,128]{2,0,1:T(1,128)} %param.12) | copy-start | bytes 7684
  1.3 0.9 %copy-start = (bf16[512,256]{1,0:T(8,128)(2,1)S(1)}, bf16[512,256]{1,0:T(8,128)(2,1)}, u32[]{:S(2)}) copy-start(bf16[512,256]{1,0:T(8,128)(2,1)} %feat_ref.1) | copy-start | bytes 786436
  2.3 0.9 %copy-start.1 = (bf16[512,256]{1,0:T(8,128)(2,1)S(1)}, bf16[512,256]{1,0:T(8,128)(2,1)}, u32[]{:S(2)}) copy-start(bf16[512,256]{1,0:T(8,128)(2,1)} %up_ref.1) | copy-start | bytes 786436
  3.2 0.9 %copy-start.2 = (bf16[256,256]{1,0:T(8,128)(2,1)S(1)}, bf16[256,256]{1,0:T(8,128)(2,1)}, u32[]{:S(2)}) copy-start(bf16[256,256]{1,0:T(8,128)(2,1)} %w_self_ref.1) | copy-start | bytes 393220
  4.1 0.9 %copy-start.3 = (bf16[256,256]{1,0:T(8,128)(2,1)S(1)}, bf16[256,256]{1,0:T(8,128)(2,1)}, u32[]{:S(2)}) copy-start(bf16[256,256]{1,0:T(8,128)(2,1)} %w_neigh_ref.1) | copy-start | bytes 393220
  5.0 0.8 %copy-start.4 = (s32[512,10]{0,1:T(8,128)S(1)}, s32[512,10]{0,1:T(8,128)}, u32[]{:S(2)}) copy-start(s32[512,10]{0,1:T(8,128)} %param.10) | copy-start | bytes 61444
  5.8 0.7 %copy-start.6 = (s32[512]{0:T(512)S(1)}, s32[512]{0:T(512)}, u32[]{:S(2)}) copy-start(s32[512]{0:T(512)} %degree_ref.1) | copy-start | bytes 6148

commit v2 on v1

--- a/solution.py
+++ b/solution.py
@@ -37,10 +37,11 @@
 
 def kernel(
     inner, outer, levels, bnd,
-    feat_ref, w_self_ref, w_neigh_ref, slots_ref, degree_ref, boundary_ref, up_ref,
-    hidden_ref, node_ref, step_ref,
+    feat_hbm, w_self_hbm, w_neigh_hbm, slots_hbm, degree_hbm, boundary_hbm, up_hbm,
+    hidden_ref, node_ref, gathered,
+    feat_ref, w_self_ref, w_neigh_ref, slots_ref, degree_ref, boundary_ref, up_ref, fetch_sem,
     table, pick, out_rows, in_rows, out_grads, in_grads,
-    stack, part_in, part, plane_in, gathered,
+    stack, part_in, part, plane_in,
     row_ss, row_rs, grad_ss, grad_rs, part_ss, part_rs, plane_ss, plane_rs, gather_ss, gather_rs,
 ):
     me = lax.axis_index("dom")
@@ -50,6 +51,17 @@
     chunk = stack.shape[0] // inner
     mine = lax.rem(me, inner)
 
+    fetches = [
+        pltpu.make_async_copy(src, dst, fetch_sem.at[index])
+        for index, (src, dst) in enumerate((
+            (boundary_hbm, boundary_ref), (feat_hbm, feat_ref), (degree_hbm, degree_ref),
+            (slots_hbm, slots_ref), (w_self_hbm, w_self_ref), (w_neigh_hbm, w_neigh_ref),
+            (up_hbm, up_ref),
+        ))
+    ]
+    for fetch in fetches:
+        fetch.start()
+
     inner_masks = list(range(1, inner))
     outer_masks = [e * inner for e in range(1, outer)]
     barrier = pltpu.get_barrier_semaphore()
@@ -64,6 +76,8 @@
             device_id=(partner(me, mask),), device_id_type=pl.DeviceIdType.MESH,
         )
 
+    fetches[0].wait()
+    fetches[1].wait()
     feat = feat_ref[...]
 
     row_id = lax.broadcasted_iota(jnp.int32, (nodes, bnd), 0)
@@ -80,6 +94,8 @@
         )
         row_copies[level].start()
 
+    fetches[2].wait()
+    fetches[3].wait()
     degree_row = degree_ref[...].reshape(1, nodes)
     named = [
         jnp.where(degree_row > slot, slots_ref[slot : slot + 1, :], -1) for slot in range(slot_count)
@@ -101,6 +117,8 @@
     share = jnp.concatenate([share] * (feat.shape[1] // 128), axis=1)
 
     summed = dot_rows(table[:nodes, :], feat)
+    for fetch in fetches[4:]:
+        fetch.wait()
     pre_self = dot(feat, w_self_ref[...])
     for level in range(levels):
         row_copies[level].wait_recv()
@@ -172,11 +190,23 @@
         gather_copies.append(copy)
     for copy in gather_copies:
         copy.wait_recv()
-    whole = gathered[...].astype(jnp.float32)
-    step_ref[...] = whole * lax.rsqrt(jnp.mean(whole * whole) + epsilon)
-
     for copy in row_copies + part_copies + grad_copies + plane_copies + gather_copies:
         copy.wait_send()
+
+
+def finish(hidden, node, gathered, hidden_hbm, node_hbm, step_hbm, step, sems):
+    copies = [
+        pltpu.make_async_copy(hidden, hidden_hbm, sems.at[0]),
+        pltpu.make_async_copy(node, node_hbm, sems.at[1]),
+        pltpu.make_async_copy(step, step_hbm, sems.at[2]),
+    ]
+    copies[0].start()
+    copies[1].start()
+    whole = gathered[...].astype(jnp.float32)
+    step[...] = whole * lax.rsqrt(jnp.mean(whole * whole) + epsilon)
+    copies[2].start()
+    for copy in copies:
+        copy.wait()
 
 
 def per_device(features, w_self, w_neigh, neighbors, degree, boundary, upstream):
@@ -191,16 +221,20 @@
     bf16 = jnp.bfloat16
     sem = pltpu.SemaphoreType.DMA
     vmem = pl.BlockSpec(memory_space=pltpu.VMEM)
-    return pl.pallas_call(
+    hbm = pl.BlockSpec(memory_space=pltpu.HBM)
+    args = (features, w_self, w_neigh, neighbors.T, degree, boundary.transpose(1, 0, 2), upstream)
+    args = tuple(pltpu.with_memory_space_constraint(arg, pltpu.HBM) for arg in args)
+    hidden, node, gathered = pl.pallas_call(
         functools.partial(kernel, inner, outer, levels, bnd),
         out_shape=(
-            jax.ShapeDtypeStruct((nodes, width), bf16),
-            jax.ShapeDtypeStruct((nodes, width), bf16),
-            jax.ShapeDtypeStruct((2 * width, width), jnp.float32),
-        ),
-        in_specs=[vmem] * 7,
+            pltpu.VMEM((nodes, width), bf16),
+            pltpu.VMEM((nodes, width), bf16),
+            pltpu.VMEM((2 * width, width), bf16),
+        ),
+        in_specs=[hbm] * 7,
         out_specs=(vmem, vmem, vmem),
-        scratch_shapes=[
+        scratch_shapes=[pltpu.VMEM(arg.shape, arg.dtype) for arg in args] + [
+            sem((7,)),
             pltpu.VMEM((nodes + rows, nodes), bf16),
             pltpu.VMEM((nodes, rows), bf16),
             pltpu.VMEM((rows, width), bf16),
@@ -211,7 +245,6 @@
             pltpu.VMEM((inner, chunk, width), bf16),
             pltpu.VMEM((chunk, width), bf16),
             pltpu.VMEM((outer, chunk, width), bf16),
-            pltpu.VMEM((2 * width, width), bf16),
             sem((levels,)), sem((levels,)), sem((levels,)), sem((levels,)),
             sem((inner,)), sem((inner,)), sem((outer,)), sem((outer,)), sem((inner,)), sem((inner,)),
         ],
@@ -219,7 +252,20 @@
             collective_id=0, has_side_effects=True, vmem_limit_bytes=40 << 20
         ),
         cost_estimate=pl.CostEstimate(flops=1 << 30, bytes_accessed=3 << 20, transcendentals=nodes * width),
-    )(features, w_self, w_neigh, neighbors.T, degree, boundary.transpose(1, 0, 2), upstream)
+    )(*args)
+    return pl.pallas_call(
+        finish,
+        out_shape=(
+            jax.ShapeDtypeStruct((nodes, width), bf16),
+            jax.ShapeDtypeStruct((nodes, width), bf16),
+            jax.ShapeDtypeStruct((2 * width, width), jnp.float32),
+        ),
+        in_specs=[vmem] * 3,
+        out_specs=(hbm, hbm, hbm),
+        scratch_shapes=[pltpu.VMEM((2 * width, width), jnp.float32), sem((3,))],
+        compiler_params=pltpu.CompilerParams(vmem_limit_bytes=16 << 20),
+        cost_estimate=pl.CostEstimate(flops=1 << 18, bytes_accessed=1 << 20, transcendentals=0),
+    )(hidden, node, gathered)
 
 
 def solution(mesh):

time: 36.2 us -> 29 us (0.80)
  local copies, waits for them, and re-layouts: 8.02 us -> 0 us
  Pallas kernels: 27.2 us -> 28.2 us
    unnamed x17 -> x0, local copies, waits for them, and re-layouts: 8.02 us -> none
    pallas_call x0 -> x1, Pallas kernels: none -> 1.15 us  [per_device(): pl.pallas_call(finish, out_shape=(jax.ShapeDtypeStruct((nodes, width), bf...]
where the time goes in v2:
time: 29 us; the launch traced here: 28.8 us
  Pallas kernels  28.2 us (97%)
  between operations  0.64 us (2%)
    pallas_call x1, Pallas kernels, per_device(): pl.pallas_call(functools.partial(kernel, inner, outer, levels, bnd), out_...  27.1 us
    pallas_call x1, Pallas kernels, per_device(): pl.pallas_call(finish, out_shape=(jax.ShapeDtypeStruct((nodes, width), bf...  1.15 us

profile of v2, /device:TPU:0, one launch (start us, length us, event | category | flops | bytes accessed | tf_op | source)
XLA Modules:
  0.0 28.8 jit_solution(3872543674854530281)
XLA Ops:
  0.6 27.1 %shard_map.94 = (bf16[512,256]{1,0:T(8,128)(2,1)S(1)}, bf16[512,256]{1,0:T(8,128)(2,1)S(1)}, bf16[512,256]{1,0:T(8,128)(2,1)S(1)}) custom-call(bf16[512,256]{1,0:T(8,128)(2,1)} %feat_hbm.1, bf16[256,256]{1,0:T(8,128)(2,1)} %w_self_hbm.1, bf16[256,256]{1,0:T(8,128)(2,1)} %w_neigh_hbm.1, s32[10,512]{1,0:T(8,128)} %bitcast.2, s32[512]{0:T(512)} %degree_hbm.1, ...), custom_call_target="tpu_custom_call" | custom-call | flops 1073741824 | bytes 3145728 | tf_op jit(solution)/shard_map/pallas_call | solution.py:227
  27.7 1.1 %shard_map.95 = (bf16[512,256]{1,0:T(8,128)(2,1)}, bf16[512,256]{1,0:T(8,128)(2,1)}, f32[512,256]{1,0:T(8,128)}) custom-call(bf16[512,256]{1,0:T(8,128)(2,1)S(1)} %get-tuple-element.6.hidden, bf16[512,256]{1,0:T(8,128)(2,1)S(1)} %get-tuple-element.7.node, bf16[512,256]{1,0:T(8,128)(2,1)S(1)} %get-tuple-element.8.gathered), custom_call_target="tpu_custom_call" | custom-call | flops 262144 | bytes 1048576 | tf_op jit(solution)/shard_map/pallas_call | solution.py:256

commit v3 on v2

--- a/solution.py
+++ b/solution.py
@@ -48,7 +48,7 @@
     nodes = feat_ref.shape[0]
     slot_count = slots_ref.shape[0]
     total_rows = table.shape[0]
-    chunk = stack.shape[0] // inner
+    chunk = stack.shape[1] // inner
     mine = lax.rem(me, inner)
 
     fetches = [
@@ -132,64 +132,81 @@
     ).astype(jnp.bfloat16)
 
     width = feat.shape[1]
-    stack[:width, :] = dot_rows(feat, pre_grad).astype(jnp.bfloat16)
-    stack[width:, :] = dot_rows(agg, pre_grad).astype(jnp.bfloat16)
     part_copies = []
-    for mask in inner_masks:
-        theirs = lax.rem(partner(me, mask), inner)
-        copy = remote(
-            stack.at[pl.ds(pl.multiple_of(theirs * chunk, chunk), chunk), :],
-            part_in.at[mask], part_ss.at[mask], part_rs.at[mask], mask,
-        )
-        copy.start()
-        part_copies.append(copy)
+    for half, left in enumerate((feat, agg)):
+        stack[half] = dot_rows(left, pre_grad).astype(jnp.bfloat16)
+        for mask in inner_masks:
+            theirs = lax.rem(partner(me, mask), inner)
+            copy = remote(
+                stack.at[half, pl.ds(pl.multiple_of(theirs * chunk, chunk), chunk), :],
+                part_in.at[half, mask], part_ss.at[half, mask], part_rs.at[half, mask], mask,
+            )
+            copy.start()
+            part_copies.append(copy)
 
     slot_share = (dot_cols(pre_grad, w_neigh_ref[...]) * share).astype(jnp.bfloat16)
     out_grads[...] = dot(table[nodes:, :], slot_share).astype(jnp.bfloat16)
     grad_copies = []
-    for level in reversed(range(levels)):
+
+    def return_grads(level):
         span = pl.ds(level * bnd, bnd)
         copy = remote(
             out_grads.at[span, :], in_grads.at[span, :], grad_ss.at[level], grad_rs.at[level], 1 << level
         )
         copy.start()
         grad_copies.append(copy)
+
+    inner_levels = inner.bit_length() - 1
+    for level in range(inner_levels):
+        return_grads(level)
     local = dot_cols(pre_grad, w_self_ref[...]) + dot(table[:nodes, :], slot_share)
 
     own = pl.ds(pl.multiple_of(mine * chunk, chunk), chunk)
-    for copy in part_copies:
-        copy.wait_recv()
-    total = stack[own, :].astype(jnp.float32)
-    for mask in inner_masks:
-        total = total + part_in[mask].astype(jnp.float32)
-    part[...] = total.astype(jnp.bfloat16)
+    per_half = len(inner_masks)
     plane_copies = []
-    for index, mask in enumerate(outer_masks):
-        copy = remote(part, plane_in.at[index + 1], plane_ss.at[index + 1], plane_rs.at[index + 1], mask)
-        copy.start()
-        plane_copies.append(copy)
+    for half in range(2):
+        for copy in part_copies[half * per_half : (half + 1) * per_half]:
+            copy.wait_recv()
+        total = stack[half, own, :].astype(jnp.float32)
+        for mask in inner_masks:
+            total = total + part_in[half, mask].astype(jnp.float32)
+        part[half] = total.astype(jnp.bfloat16)
+        for index, mask in enumerate(outer_masks):
+            copy = remote(
+                part.at[half], plane_in.at[half, index + 1],
+                plane_ss.at[half, index + 1], plane_rs.at[half, index + 1], mask,
+            )
+            copy.start()
+            plane_copies.append(copy)
+    for level in range(inner_levels, levels):
+        return_grads(level)
+
+    per_outer = len(outer_masks)
+    gather_copies = []
+    for half in range(2):
+        for copy in plane_copies[half * per_outer : (half + 1) * per_outer]:
+            copy.wait_recv()
+        terms = [part[half].astype(jnp.float32)]
+        for index in range(1, outer):
+            terms.append(plane_in[half, index].astype(jnp.float32))
+        while len(terms) > 1:
+            terms = [terms[i] + terms[i + 1] for i in range(0, len(terms), 2)]
+        rows = pl.ds(pl.multiple_of(half * width + mine * chunk, chunk), chunk)
+        gathered[rows, :] = terms[0].astype(jnp.bfloat16)
+        for mask in inner_masks:
+            copy = remote(
+                gathered.at[rows, :], gathered.at[rows, :],
+                gather_ss.at[half, mask], gather_rs.at[half, mask], mask,
+            )
+            copy.start()
+            gather_copies.append(copy)
 
     for copy in grad_copies:
         copy.wait_recv()
     node_ref[...] = (local + dot(pick[...], in_grads[...])).astype(jnp.bfloat16)
-
-    for copy in plane_copies:
-        copy.wait_recv()
-    terms = [part[...].astype(jnp.float32)]
-    for index in range(1, outer):
-        terms.append(plane_in[index].astype(jnp.float32))
-    while len(terms) > 1:
-        terms = [terms[i] + terms[i + 1] for i in range(0, len(terms), 2)]
-    gathered[own, :] = terms[0].astype(jnp.bfloat16)
-    gather_copies = []
-    for mask in inner_masks:
-        copy = remote(
-            gathered.at[own, :], gathered.at[own, :], gather_ss.at[mask], gather_rs.at[mask], mask
-        )
-        copy.start()
-        gather_copies.append(copy)
     for copy in gather_copies:
         copy.wait_recv()
+
     for copy in row_copies + part_copies + grad_copies + plane_copies + gather_copies:
         copy.wait_send()
 
@@ -217,7 +234,7 @@
     nodes, width = features.shape
     bnd = boundary.shape[2]
     rows = levels * bnd
-    chunk = 2 * width // inner
+    chunk = width // inner
     bf16 = jnp.bfloat16
     sem = pltpu.SemaphoreType.DMA
     vmem = pl.BlockSpec(memory_space=pltpu.VMEM)
@@ -241,12 +258,12 @@
             pltpu.VMEM((rows, width), bf16),
             pltpu.VMEM((rows, width), bf16),
             pltpu.VMEM((rows, width), bf16),
-            pltpu.VMEM((2 * width, width), bf16),
-            pltpu.VMEM((inner, chunk, width), bf16),
-            pltpu.VMEM((chunk, width), bf16),
-            pltpu.VMEM((outer, chunk, width), bf16),
+            pltpu.VMEM((2, width, width), bf16),
+            pltpu.VMEM((2, inner, chunk, width), bf16),
+            pltpu.VMEM((2, chunk, width), bf16),
+            pltpu.VMEM((2, outer, chunk, width), bf16),
             sem((levels,)), sem((levels,)), sem((levels,)), sem((levels,)),
-            sem((inner,)), sem((inner,)), sem((outer,)), sem((outer,)), sem((inner,)), sem((inner,)),
+            sem((2, inner)), sem((2, inner)), sem((2, outer)), sem((2, outer)), sem((2, inner)), sem((2, inner)),
         ],
         compiler_params=pltpu.CompilerParams(
             collective_id=0, has_side_effects=True, vmem_limit_bytes=40 << 20

time: 29 us -> 27.5 us (0.948)
  Pallas kernels: 28.2 us -> 26.7 us
    pallas_call x1, Pallas kernels: 27.1 us -> 25.5 us  [per_device(): pl.pallas_call(functools.partial(kernel, inner, outer, levels, bnd), out_...]
where the time goes in v3:
time: 27.5 us; the launch traced here: 27.3 us
  Pallas kernels  26.7 us (97%)
  between operations  0.64 us (2%)
    pallas_call x1, Pallas kernels, per_device(): pl.pallas_call(functools.partial(kernel, inner, outer, levels, bnd), out_...  25.5 us
    pallas_call x1, Pallas kernels, per_device(): pl.pallas_call(finish, out_shape=(jax.ShapeDtypeStruct((nodes, width), bf...  1.15 us

profile of v3, /device:TPU:0, one launch (start us, length us, event | category | flops | bytes accessed | tf_op | source)
XLA Modules:
  0.0 27.3 jit_solution(2121797526085065774)
XLA Ops:
  0.6 25.5 %shard_map.94 = (bf16[512,256]{1,0:T(8,128)(2,1)S(1)}, bf16[512,256]{1,0:T(8,128)(2,1)S(1)}, bf16[512,256]{1,0:T(8,128)(2,1)S(1)}) custom-call(bf16[512,256]{1,0:T(8,128)(2,1)} %feat_hbm.1, bf16[256,256]{1,0:T(8,128)(2,1)} %w_self_hbm.1, bf16[256,256]{1,0:T(8,128)(2,1)} %w_neigh_hbm.1, s32[10,512]{1,0:T(8,128)} %bitcast.2, s32[512]{0:T(512)} %degree_hbm.1, ...), custom_call_target="tpu_custom_call" | custom-call | flops 1073741824 | bytes 3145728 | tf_op jit(solution)/shard_map/pallas_call | solution.py:244
  26.2 1.1 %shard_map.95 = (bf16[512,256]{1,0:T(8,128)(2,1)}, bf16[512,256]{1,0:T(8,128)(2,1)}, f32[512,256]{1,0:T(8,128)}) custom-call(bf16[512,256]{1,0:T(8,128)(2,1)S(1)} %get-tuple-element.6.hidden, bf16[512,256]{1,0:T(8,128)(2,1)S(1)} %get-tuple-element.7.node, bf16[512,256]{1,0:T(8,128)(2,1)S(1)} %get-tuple-element.8.gathered), custom_call_target="tpu_custom_call" | custom-call | flops 262144 | bytes 1048576 | tf_op jit(solution)/shard_map/pallas_call | solution.py:273

commit v4 on v3

--- a/solution.py
+++ b/solution.py
@@ -9,7 +9,7 @@
 
 epsilon = 1e-06
 INNER_BITS = 3
-BUILD_ROWS = 64
+BUILD_ROWS = 128
 
 
 def partner(me, mask):
@@ -40,7 +40,7 @@
     feat_hbm, w_self_hbm, w_neigh_hbm, slots_hbm, degree_hbm, boundary_hbm, up_hbm,
     hidden_ref, node_ref, gathered,
     feat_ref, w_self_ref, w_neigh_ref, slots_ref, degree_ref, boundary_ref, up_ref, fetch_sem,
-    table, pick, out_rows, in_rows, out_grads, in_grads,
+    table, table_t, pick, out_rows, in_rows, out_grads, in_grads,
     stack, part_in, part, plane_in,
     row_ss, row_rs, grad_ss, grad_rs, part_ss, part_rs, plane_ss, plane_rs, gather_ss, gather_rs,
 ):
@@ -101,13 +101,16 @@
         jnp.where(degree_row > slot, slots_ref[slot : slot + 1, :], -1) for slot in range(slot_count)
     ]
 
+    named = jnp.concatenate(named, axis=0).astype(jnp.float32)
+    row = lax.broadcasted_iota(jnp.int32, (BUILD_ROWS, nodes), 0).astype(jnp.float32).astype(jnp.bfloat16)
+
     def build(block, carry):
         start = pl.multiple_of(block * BUILD_ROWS, BUILD_ROWS)
-        row = lax.broadcasted_iota(jnp.int32, (BUILD_ROWS, nodes), 0) + start
-        count = jnp.zeros((BUILD_ROWS, nodes), jnp.float32)
+        shifted = (named - start.astype(jnp.float32)).astype(jnp.bfloat16)
+        count = jnp.zeros((BUILD_ROWS, nodes), jnp.bfloat16)
         for slot in range(slot_count):
-            count = jnp.where(row == named[slot], count + 1.0, count)
-        table[pl.ds(start, BUILD_ROWS), :] = count.astype(jnp.bfloat16)
+            count = jnp.where(row == shifted[slot : slot + 1, :], count + 1, count)
+        table[pl.ds(start, BUILD_ROWS), :] = count
         return carry
 
     lax.fori_loop(0, total_rows // BUILD_ROWS, build, 0)
@@ -116,13 +119,20 @@
     share = jnp.transpose(jnp.broadcast_to(share_row, (128, nodes)))
     share = jnp.concatenate([share] * (feat.shape[1] // 128), axis=1)
 
+    table_t[...] = jnp.transpose(table[nodes:, :])
+    feat_t = jnp.transpose(feat)
     summed = dot_rows(table[:nodes, :], feat)
     for fetch in fetches[4:]:
         fetch.wait()
     pre_self = dot(feat, w_self_ref[...])
-    for level in range(levels):
+    inner_levels = inner.bit_length() - 1
+    near = inner_levels * bnd
+    for level in range(inner_levels):
         row_copies[level].wait_recv()
-    summed = summed + dot_rows(table[nodes:, :], in_rows[...])
+    summed = summed + dot(table_t[:, :near], in_rows[:near, :])
+    for level in range(inner_levels, levels):
+        row_copies[level].wait_recv()
+    summed = summed + dot(table_t[:, near:], in_rows[near:, :])
     agg = (summed * share).astype(jnp.bfloat16)
     pre_sum = pre_self + dot(agg, w_neigh_ref[...])
     sigmoid = jax.nn.sigmoid(pre_sum)
@@ -133,8 +143,9 @@
 
     width = feat.shape[1]
     part_copies = []
-    for half, left in enumerate((feat, agg)):
-        stack[half] = dot_rows(left, pre_grad).astype(jnp.bfloat16)
+    for half in range(2):
+        left_t = feat_t if half == 0 else jnp.transpose(agg)
+        stack[half] = dot(left_t, pre_grad).astype(jnp.bfloat16)
         for mask in inner_masks:
             theirs = lax.rem(partner(me, mask), inner)
             copy = remote(
@@ -156,7 +167,6 @@
         copy.start()
         grad_copies.append(copy)
 
-    inner_levels = inner.bit_length() - 1
     for level in range(inner_levels):
         return_grads(level)
     local = dot_cols(pre_grad, w_self_ref[...]) + dot(table[:nodes, :], slot_share)
@@ -253,6 +263,7 @@
         scratch_shapes=[pltpu.VMEM(arg.shape, arg.dtype) for arg in args] + [
             sem((7,)),
             pltpu.VMEM((nodes + rows, nodes), bf16),
+            pltpu.VMEM((nodes, rows), bf16),
             pltpu.VMEM((nodes, rows), bf16),
             pltpu.VMEM((rows, width), bf16),
             pltpu.VMEM((rows, width), bf16),

time: 27.5 us -> 27.2 us (0.989)
  Pallas kernels: 26.7 us -> 26.4 us
    pallas_call x1, Pallas kernels: 25.5 us -> 25.2 us  [per_device(): pl.pallas_call(functools.partial(kernel, inner, outer, levels, bnd), out_...]
where the time goes in v4:
time: 27.2 us; the launch traced here: 27 us
  Pallas kernels  26.4 us (97%)
  between operations  0.64 us (2%)
    pallas_call x1, Pallas kernels, per_device(): pl.pallas_call(functools.partial(kernel, inner, outer, levels, bnd), out_...  25.2 us
    pallas_call x1, Pallas kernels, per_device(): pl.pallas_call(finish, out_shape=(jax.ShapeDtypeStruct((nodes, width), bf...  1.15 us

profile of v4, /device:TPU:0, one launch (start us, length us, event | category | flops | bytes accessed | tf_op | source)
XLA Modules:
  0.0 27.0 jit_solution(8981864752314907402)
XLA Ops:
  0.6 25.2 %shard_map.94 = (bf16[512,256]{1,0:T(8,128)(2,1)S(1)}, bf16[512,256]{1,0:T(8,128)(2,1)S(1)}, bf16[512,256]{1,0:T(8,128)(2,1)S(1)}) custom-call(bf16[512,256]{1,0:T(8,128)(2,1)} %feat_hbm.1, bf16[256,256]{1,0:T(8,128)(2,1)} %w_self_hbm.1, bf16[256,256]{1,0:T(8,128)(2,1)} %w_neigh_hbm.1, s32[10,512]{1,0:T(8,128)} %bitcast.2, s32[512]{0:T(512)} %degree_hbm.1, ...), custom_call_target="tpu_custom_call" | custom-call | flops 1073741824 | bytes 3145728 | tf_op jit(solution)/shard_map/pallas_call | solution.py:254
  25.9 1.1 %shard_map.95 = (bf16[512,256]{1,0:T(8,128)(2,1)}, bf16[512,256]{1,0:T(8,128)(2,1)}, f32[512,256]{1,0:T(8,128)}) custom-call(bf16[512,256]{1,0:T(8,128)(2,1)S(1)} %get-tuple-element.6.hidden, bf16[512,256]{1,0:T(8,128)(2,1)S(1)} %get-tuple-element.7.node, bf16[512,256]{1,0:T(8,128)(2,1)S(1)} %get-tuple-element.8.gathered), custom_call_target="tpu_custom_call" | custom-call | flops 262144 | bytes 1048576 | tf_op jit(solution)/shard_map/pallas_call | solution.py:284

commit v5 on v4

--- a/solution.py
+++ b/solution.py
@@ -65,7 +65,9 @@
     inner_masks = list(range(1, inner))
     outer_masks = [e * inner for e in range(1, outer)]
     barrier = pltpu.get_barrier_semaphore()
-    for mask in inner_masks + outer_masks:
+    greeted = [1 << level for level in range(levels)]
+    greeted += [mask for mask in inner_masks + outer_masks if mask.bit_count() > 2]
+    for mask in greeted:
         pl.semaphore_signal(
             barrier, inc=1, device_id=(partner(me, mask),), device_id_type=pl.DeviceIdType.MESH
         )
@@ -88,7 +90,7 @@
         pick[:, span] = hot
         out_rows[span, :] = dot_rows(hot, feat).astype(jnp.bfloat16)
         if place == 0:
-            pl.semaphore_wait(barrier, len(inner_masks) + len(outer_masks))
+            pl.semaphore_wait(barrier, len(greeted))
         row_copies[level] = remote(
             out_rows.at[span, :], in_rows.at[span, :], row_ss.at[level], row_rs.at[level], 1 << level
         )
@@ -167,7 +169,7 @@
         copy.start()
         grad_copies.append(copy)
 
-    for level in range(inner_levels):
+    for level in reversed(range(levels)):
         return_grads(level)
     local = dot_cols(pre_grad, w_self_ref[...]) + dot(table[:nodes, :], slot_share)
 
@@ -188,8 +190,6 @@
             )
             copy.start()
             plane_copies.append(copy)
-    for level in range(inner_levels, levels):
-        return_grads(level)
 
     per_outer = len(outer_masks)
     gather_copies = []

time: 27.2 us -> 27 us (level)
  no operation moved by 1% of the time
where the time goes in v5:
time: 27 us; the launch traced here: 26.8 us
  Pallas kernels  26.2 us (97%)
  between operations  0.64 us (2%)
    pallas_call x1, Pallas kernels, per_device(): pl.pallas_call(functools.partial(kernel, inner, outer, levels, bnd), out_...  25 us
    pallas_call x1, Pallas kernels, per_device(): pl.pallas_call(finish, out_shape=(jax.ShapeDtypeStruct((nodes, width), bf...  1.15 us

profile of v5, /device:TPU:0, one launch (start us, length us, event | category | flops | bytes accessed | tf_op | source)
XLA Modules:
  0.0 26.8 jit_solution(13415721919946766285)
XLA Ops:
  0.6 25.0 %shard_map.94 = (bf16[512,256]{1,0:T(8,128)(2,1)S(1)}, bf16[512,256]{1,0:T(8,128)(2,1)S(1)}, bf16[512,256]{1,0:T(8,128)(2,1)S(1)}) custom-call(bf16[512,256]{1,0:T(8,128)(2,1)} %feat_hbm.1, bf16[256,256]{1,0:T(8,128)(2,1)} %w_self_hbm.1, bf16[256,256]{1,0:T(8,128)(2,1)} %w_neigh_hbm.1, s32[10,512]{1,0:T(8,128)} %bitcast.2, s32[512]{0:T(512)} %degree_hbm.1, ...), custom_call_target="tpu_custom_call" | custom-call | flops 1073741824 | bytes 3145728 | tf_op jit(solution)/shard_map/pallas_call | solution.py:254
  25.6 1.1 %shard_map.95 = (bf16[512,256]{1,0:T(8,128)(2,1)}, bf16[512,256]{1,0:T(8,128)(2,1)}, f32[512,256]{1,0:T(8,128)}) custom-call(bf16[512,256]{1,0:T(8,128)(2,1)S(1)} %get-tuple-element.6.hidden, bf16[512,256]{1,0:T(8,128)(2,1)S(1)} %get-tuple-element.7.node, bf16[512,256]{1,0:T(8,128)(2,1)S(1)} %get-tuple-element.8.gathered), custom_call_target="tpu_custom_call" | custom-call | flops 262144 | bytes 1048576 | tf_op jit(solution)/shard_map/pallas_call | solution.py:284

commit v6 on v5

--- a/solution.py
+++ b/solution.py
@@ -40,7 +40,7 @@
     feat_hbm, w_self_hbm, w_neigh_hbm, slots_hbm, degree_hbm, boundary_hbm, up_hbm,
     hidden_ref, node_ref, gathered,
     feat_ref, w_self_ref, w_neigh_ref, slots_ref, degree_ref, boundary_ref, up_ref, fetch_sem,
-    table, table_t, pick, out_rows, in_rows, out_grads, in_grads,
+    feat_t, table, pick, out_rows, in_rows, out_grads, in_grads,
     stack, part_in, part, plane_in,
     row_ss, row_rs, grad_ss, grad_rs, part_ss, part_rs, plane_ss, plane_rs, gather_ss, gather_rs,
 ):
@@ -80,21 +80,22 @@
 
     fetches[0].wait()
     fetches[1].wait()
-    feat = feat_ref[...]
+    feat_t[...] = jnp.transpose(feat_ref[...])
 
     row_id = lax.broadcasted_iota(jnp.int32, (nodes, bnd), 0)
-    row_copies = [None] * levels
-    for place, level in enumerate(reversed(range(levels))):
+    for level in range(levels):
         hot = (row_id == boundary_ref[level]).astype(jnp.float32).astype(jnp.bfloat16)
-        span = pl.ds(level * bnd, bnd)
-        pick[:, span] = hot
-        out_rows[span, :] = dot_rows(hot, feat).astype(jnp.bfloat16)
-        if place == 0:
-            pl.semaphore_wait(barrier, len(greeted))
-        row_copies[level] = remote(
-            out_rows.at[span, :], in_rows.at[span, :], row_ss.at[level], row_rs.at[level], 1 << level
-        )
-        row_copies[level].start()
+        pick[:, pl.ds(level * bnd, bnd)] = hot
+    picked = dot(feat_t[...], pick[...]).astype(jnp.bfloat16)
+    for level in range(levels):
+        out_rows[level] = picked[:, level * bnd : (level + 1) * bnd]
+    pl.semaphore_wait(barrier, len(greeted))
+    row_copies = [
+        remote(out_rows.at[level], in_rows.at[level], row_ss.at[level], row_rs.at[level], 1 << level)
+        for level in range(levels)
+    ]
+    for copy in reversed(row_copies):
+        copy.start()
 
     fetches[2].wait()
     fetches[3].wait()
@@ -117,37 +118,32 @@
 
     lax.fori_loop(0, total_rows // BUILD_ROWS, build, 0)
 
-    share_row = 1.0 / degree_row.astype(jnp.float32)
-    share = jnp.transpose(jnp.broadcast_to(share_row, (128, nodes)))
-    share = jnp.concatenate([share] * (feat.shape[1] // 128), axis=1)
-
-    table_t[...] = jnp.transpose(table[nodes:, :])
-    feat_t = jnp.transpose(feat)
-    summed = dot_rows(table[:nodes, :], feat)
+    share = 1.0 / degree_row.astype(jnp.float32)
+    summed = dot(feat_t[...], table[:nodes, :])
     for fetch in fetches[4:]:
         fetch.wait()
-    pre_self = dot(feat, w_self_ref[...])
+    pre_self = dot_rows(w_self_ref[...], feat_t[...])
+    w_neigh_t = jnp.transpose(w_neigh_ref[...])
+    up_t = jnp.transpose(up_ref[...])
+
     inner_levels = inner.bit_length() - 1
-    near = inner_levels * bnd
-    for level in range(inner_levels):
-        row_copies[level].wait_recv()
-    summed = summed + dot(table_t[:, :near], in_rows[:near, :])
-    for level in range(inner_levels, levels):
-        row_copies[level].wait_recv()
-    summed = summed + dot(table_t[:, near:], in_rows[near:, :])
-    agg = (summed * share).astype(jnp.bfloat16)
-    pre_sum = pre_self + dot(agg, w_neigh_ref[...])
+    for low, high in ((0, inner_levels), (inner_levels, levels)):
+        for level in range(low, high):
+            row_copies[level].wait_recv()
+        rows_t = jnp.concatenate([in_rows[level] for level in range(low, high)], axis=1)
+        summed = summed + dot(rows_t, table[nodes + low * bnd : nodes + high * bnd, :])
+    agg_t = (summed * share).astype(jnp.bfloat16)
+    pre_sum = pre_self + dot(w_neigh_t, agg_t)
     sigmoid = jax.nn.sigmoid(pre_sum)
-    hidden_ref[...] = (pre_sum * sigmoid).astype(jnp.bfloat16)
     pre_grad = (
-        up_ref[...].astype(jnp.float32) * sigmoid * (1.0 + pre_sum * (1.0 - sigmoid))
+        up_t.astype(jnp.float32) * sigmoid * (1.0 + pre_sum * (1.0 - sigmoid))
     ).astype(jnp.bfloat16)
 
-    width = feat.shape[1]
+    width = feat_t.shape[0]
     part_copies = []
     for half in range(2):
-        left_t = feat_t if half == 0 else jnp.transpose(agg)
-        stack[half] = dot(left_t, pre_grad).astype(jnp.bfloat16)
+        left_t = feat_t[...] if half == 0 else agg_t
+        stack[half] = dot_cols(left_t, pre_grad).astype(jnp.bfloat16)
         for mask in inner_masks:
             theirs = lax.rem(partner(me, mask), inner)
             copy = remote(
@@ -157,8 +153,8 @@
             copy.start()
             part_copies.append(copy)
 
-    slot_share = (dot_cols(pre_grad, w_neigh_ref[...]) * share).astype(jnp.bfloat16)
-    out_grads[...] = dot(table[nodes:, :], slot_share).astype(jnp.bfloat16)
+    slot_share = (dot(w_neigh_ref[...], pre_grad) * share).astype(jnp.bfloat16)
+    out_grads[...] = dot_cols(table[nodes:, :], slot_share).astype(jnp.bfloat16)
     grad_copies = []
 
     def return_grads(level):
@@ -171,7 +167,8 @@
 
     for level in reversed(range(levels)):
         return_grads(level)
-    local = dot_cols(pre_grad, w_self_ref[...]) + dot(table[:nodes, :], slot_share)
+    hidden_ref[...] = jnp.transpose((pre_sum * sigmoid).astype(jnp.bfloat16))
+    local = jnp.transpose(dot(w_self_ref[...], pre_grad)) + dot_cols(table[:nodes, :], slot_share)
 
     own = pl.ds(pl.multiple_of(mine * chunk, chunk), chunk)
     per_half = len(inner_masks)
@@ -262,11 +259,11 @@
         out_specs=(vmem, vmem, vmem),
         scratch_shapes=[pltpu.VMEM(arg.shape, arg.dtype) for arg in args] + [
             sem((7,)),
+            pltpu.VMEM((width, nodes), bf16),
             pltpu.VMEM((nodes + rows, nodes), bf16),
             pltpu.VMEM((nodes, rows), bf16),
-            pltpu.VMEM((nodes, rows), bf16),
-            pltpu.VMEM((rows, width), bf16),
-            pltpu.VMEM((rows, width), bf16),
+            pltpu.VMEM((levels, width, bnd), bf16),
+            pltpu.VMEM((levels, width, bnd), bf16),
             pltpu.VMEM((rows, width), bf16),
             pltpu.VMEM((rows, width), bf16),
             pltpu.VMEM((2, width, width), bf16),

time: 27 us -> 27.1 us (level)
  no operation moved by 1% of the time
where the time goes in v6:
time: 27.1 us; the launch traced here: 26.9 us
  Pallas kernels  26.2 us (97%)
  between operations  0.64 us (2%)
    pallas_call x1, Pallas kernels, per_device(): pl.pallas_call(functools.partial(kernel, inner, outer, levels, bnd), out_...  25.1 us
    pallas_call x1, Pallas kernels, per_device(): pl.pallas_call(finish, out_shape=(jax.ShapeDtypeStruct((nodes, width), bf...  1.15 us

profile of v6, /device:TPU:0, one launch (start us, length us, event | category | flops | bytes accessed | tf_op | source)
XLA Modules:
  0.0 26.9 jit_solution(17143742894866373516)
XLA Ops:
  0.6 25.1 %shard_map.94 = (bf16[512,256]{1,0:T(8,128)(2,1)S(1)}, bf16[512,256]{1,0:T(8,128)(2,1)S(1)}, bf16[512,256]{1,0:T(8,128)(2,1)S(1)}) custom-call(bf16[512,256]{1,0:T(8,128)(2,1)} %feat_hbm.1, bf16[256,256]{1,0:T(8,128)(2,1)} %w_self_hbm.1, bf16[256,256]{1,0:T(8,128)(2,1)} %w_neigh_hbm.1, s32[10,512]{1,0:T(8,128)} %bitcast.2, s32[512]{0:T(512)} %degree_hbm.1, ...), custom_call_target="tpu_custom_call" | custom-call | flops 1073741824 | bytes 3145728 | tf_op jit(solution)/shard_map/pallas_call | solution.py:251
  25.7 1.1 %shard_map.95 = (bf16[512,256]{1,0:T(8,128)(2,1)}, bf16[512,256]{1,0:T(8,128)(2,1)}, f32[512,256]{1,0:T(8,128)}) custom-call(bf16[512,256]{1,0:T(8,128)(2,1)S(1)} %get-tuple-element.6.hidden, bf16[512,256]{1,0:T(8,128)(2,1)S(1)} %get-tuple-element.7.node, bf16[512,256]{1,0:T(8,128)(2,1)S(1)} %get-tuple-element.8.gathered), custom_call_target="tpu_custom_call" | custom-call | flops 262144 | bytes 1048576 | tf_op jit(solution)/shard_map/pallas_call | solution.py:281

commit v7 on v6

--- a/solution.py
+++ b/solution.py
@@ -62,8 +62,8 @@
     for fetch in fetches:
         fetch.start()
 
-    inner_masks = list(range(1, inner))
-    outer_masks = [e * inner for e in range(1, outer)]
+    inner_masks = list(range(inner - 1, 0, -1))
+    outer_masks = [e * inner for e in range(outer - 1, 0, -1)]
     barrier = pltpu.get_barrier_semaphore()
     greeted = [1 << level for level in range(levels)]
     greeted += [mask for mask in inner_masks + outer_masks if mask.bit_count() > 2]
@@ -165,7 +165,7 @@
         copy.start()
         grad_copies.append(copy)
 
-    for level in reversed(range(levels)):
+    for level in reversed(range(inner_levels, levels)):
         return_grads(level)
     hidden_ref[...] = jnp.transpose((pre_sum * sigmoid).astype(jnp.bfloat16))
     local = jnp.transpose(dot(w_self_ref[...], pre_grad)) + dot_cols(table[:nodes, :], slot_share)
@@ -180,13 +180,17 @@
         for mask in inner_masks:
             total = total + part_in[half, mask].astype(jnp.float32)
         part[half] = total.astype(jnp.bfloat16)
-        for index, mask in enumerate(outer_masks):
+        for mask in outer_masks:
+            index = mask // inner
             copy = remote(
-                part.at[half], plane_in.at[half, index + 1],
-                plane_ss.at[half, index + 1], plane_rs.at[half, index + 1], mask,
+                part.at[half], plane_in.at[half, index],
+                plane_ss.at[half, index], plane_rs.at[half, index], mask,
             )
             copy.start()
             plane_copies.append(copy)
+
+    for level in reversed(range(inner_levels)):
+        return_grads(level)
 
     per_outer = len(outer_masks)
     gather_copies = []

time: 27.1 us -> 26.9 us (level)
  no operation moved by 1% of the time
where the time goes in v7:
time: 26.9 us; the launch traced here: 26.8 us
  Pallas kernels  26.1 us (97%)
  between operations  0.64 us (2%)
    pallas_call x1, Pallas kernels, per_device(): pl.pallas_call(functools.partial(kernel, inner, outer, levels, bnd), out_...  25 us
    pallas_call x1, Pallas kernels, per_device(): pl.pallas_call(finish, out_shape=(jax.ShapeDtypeStruct((nodes, width), bf...  1.15 us

profile of v7, /device:TPU:0, one launch (start us, length us, event | category | flops | bytes accessed | tf_op | source)
XLA Modules:
  0.0 26.8 jit_solution(4229947626536086081)
XLA Ops:
  0.6 25.0 %shard_map.94 = (bf16[512,256]{1,0:T(8,128)(2,1)S(1)}, bf16[512,256]{1,0:T(8,128)(2,1)S(1)}, bf16[512,256]{1,0:T(8,128)(2,1)S(1)}) custom-call(bf16[512,256]{1,0:T(8,128)(2,1)} %feat_hbm.1, bf16[256,256]{1,0:T(8,128)(2,1)} %w_self_hbm.1, bf16[256,256]{1,0:T(8,128)(2,1)} %w_neigh_hbm.1, s32[10,512]{1,0:T(8,128)} %bitcast.2, s32[512]{0:T(512)} %degree_hbm.1, ...), custom_call_target="tpu_custom_call" | custom-call | flops 1073741824 | bytes 3145728 | tf_op jit(solution)/shard_map/pallas_call | solution.py:255
  25.6 1.1 %shard_map.95 = (bf16[512,256]{1,0:T(8,128)(2,1)}, bf16[512,256]{1,0:T(8,128)(2,1)}, f32[512,256]{1,0:T(8,128)}) custom-call(bf16[512,256]{1,0:T(8,128)(2,1)S(1)} %get-tuple-element.6.hidden, bf16[512,256]{1,0:T(8,128)(2,1)S(1)} %get-tuple-element.7.node, bf16[512,256]{1,0:T(8,128)(2,1)S(1)} %get-tuple-element.8.gathered), custom_call_target="tpu_custom_call" | custom-call | flops 262144 | bytes 1048576 | tf_op jit(solution)/shard_map/pallas_call | solution.py:285

commit v8 on v7

--- a/solution.py
+++ b/solution.py
@@ -215,11 +215,12 @@
     for copy in grad_copies:
         copy.wait_recv()
     node_ref[...] = (local + dot(pick[...], in_grads[...])).astype(jnp.bfloat16)
+    for copy in row_copies + part_copies + grad_copies + plane_copies:
+        copy.wait_send()
+    for copy in gather_copies:
+        copy.wait_send()
     for copy in gather_copies:
         copy.wait_recv()
-
-    for copy in row_copies + part_copies + grad_copies + plane_copies + gather_copies:
-        copy.wait_send()
 
 
 def finish(hidden, node, gathered, hidden_hbm, node_hbm, step_hbm, step, sems):

time: 26.9 us -> 26.9 us (level)
  no operation moved by 1% of the time
where the time goes in v8:
time: 26.9 us; the launch traced here: 26.7 us
  Pallas kernels  26 us (97%)
  between operations  0.64 us (2%)
    pallas_call x1, Pallas kernels, per_device(): pl.pallas_call(functools.partial(kernel, inner, outer, levels, bnd), out_...  24.9 us
    pallas_call x1, Pallas kernels, per_device(): pl.pallas_call(finish, out_shape=(jax.ShapeDtypeStruct((nodes, width), bf...  1.15 us

profile of v8, /device:TPU:0, one launch (start us, length us, event | category | flops | bytes accessed | tf_op | source)
XLA Modules:
  0.0 26.7 jit_solution(6459071994831197384)
XLA Ops:
  0.6 24.9 %shard_map.94 = (bf16[512,256]{1,0:T(8,128)(2,1)S(1)}, bf16[512,256]{1,0:T(8,128)(2,1)S(1)}, bf16[512,256]{1,0:T(8,128)(2,1)S(1)}) custom-call(bf16[512,256]{1,0:T(8,128)(2,1)} %feat_hbm.1, bf16[256,256]{1,0:T(8,128)(2,1)} %w_self_hbm.1, bf16[256,256]{1,0:T(8,128)(2,1)} %w_neigh_hbm.1, s32[10,512]{1,0:T(8,128)} %bitcast.2, s32[512]{0:T(512)} %degree_hbm.1, ...), custom_call_target="tpu_custom_call" | custom-call | flops 1073741824 | bytes 3145728 | tf_op jit(solution)/shard_map/pallas_call | solution.py:256
  25.5 1.1 %shard_map.95 = (bf16[512,256]{1,0:T(8,128)(2,1)}, bf16[512,256]{1,0:T(8,128)(2,1)}, f32[512,256]{1,0:T(8,128)}) custom-call(bf16[512,256]{1,0:T(8,128)(2,1)S(1)} %get-tuple-element.6.hidden, bf16[512,256]{1,0:T(8,128)(2,1)S(1)} %get-tuple-element.7.node, bf16[512,256]{1,0:T(8,128)(2,1)S(1)} %get-tuple-element.8.gathered), custom_call_target="tpu_custom_call" | custom-call | flops 262144 | bytes 1048576 | tf_op jit(solution)/shard_map/pallas_call | solution.py:286

commit v9 on v7

--- a/solution.py
+++ b/solution.py
@@ -41,8 +41,8 @@
     hidden_ref, node_ref, gathered,
     feat_ref, w_self_ref, w_neigh_ref, slots_ref, degree_ref, boundary_ref, up_ref, fetch_sem,
     feat_t, table, pick, out_rows, in_rows, out_grads, in_grads,
-    stack, part_in, part, plane_in,
-    row_ss, row_rs, grad_ss, grad_rs, part_ss, part_rs, plane_ss, plane_rs, gather_ss, gather_rs,
+    stack, pair_in, paired, part_in, part, plane_in,
+    pair_ss, pair_rs, row_ss, row_rs, grad_ss, grad_rs, part_ss, part_rs, plane_ss, plane_rs, gather_ss, gather_rs,
 ):
     me = lax.axis_index("dom")
     nodes = feat_ref.shape[0]
@@ -140,18 +140,11 @@
     ).astype(jnp.bfloat16)
 
     width = feat_t.shape[0]
-    part_copies = []
-    for half in range(2):
-        left_t = feat_t[...] if half == 0 else agg_t
-        stack[half] = dot_cols(left_t, pre_grad).astype(jnp.bfloat16)
-        for mask in inner_masks:
-            theirs = lax.rem(partner(me, mask), inner)
-            copy = remote(
-                stack.at[half, pl.ds(pl.multiple_of(theirs * chunk, chunk), chunk), :],
-                part_in.at[half, mask], part_ss.at[half, mask], part_rs.at[half, mask], mask,
-            )
-            copy.start()
-            part_copies.append(copy)
+    core = lax.rem(me, 2)
+    stack[0] = dot_cols(feat_t[...], pre_grad).astype(jnp.bfloat16)
+    stack[1] = dot_cols(agg_t, pre_grad).astype(jnp.bfloat16)
+    pair_copy = remote(stack.at[1 - core], pair_in, pair_ss.at[0], pair_rs.at[0], 1)
+    pair_copy.start()
 
     slot_share = (dot(w_neigh_ref[...], pre_grad) * share).astype(jnp.bfloat16)
     out_grads[...] = dot_cols(table[nodes:, :], slot_share).astype(jnp.bfloat16)
@@ -167,17 +160,32 @@
 
     for level in reversed(range(inner_levels, levels)):
         return_grads(level)
+    pair_copy.wait_recv()
+    paired[...] = (stack[core].astype(jnp.float32) + pair_in[...].astype(jnp.float32)).astype(jnp.bfloat16)
+    chip_masks = [mask for mask in inner_masks if mask % 2 == 0]
+    part_copies = []
+    for half in range(2):
+        for mask in chip_masks:
+            theirs = lax.div(lax.rem(partner(me, mask), inner), 2) * (2 * chunk) + half * chunk
+            copy = remote(
+                paired.at[pl.ds(pl.multiple_of(theirs, chunk), chunk), :],
+                part_in.at[half, mask], part_ss.at[half, mask], part_rs.at[half, mask], mask,
+            )
+            copy.start()
+            part_copies.append(copy)
+
     hidden_ref[...] = jnp.transpose((pre_sum * sigmoid).astype(jnp.bfloat16))
     local = jnp.transpose(dot(w_self_ref[...], pre_grad)) + dot_cols(table[:nodes, :], slot_share)
 
-    own = pl.ds(pl.multiple_of(mine * chunk, chunk), chunk)
-    per_half = len(inner_masks)
+    first = lax.div(mine, 2) * (2 * chunk)
+    per_half = len(chip_masks)
     plane_copies = []
     for half in range(2):
         for copy in part_copies[half * per_half : (half + 1) * per_half]:
             copy.wait_recv()
-        total = stack[half, own, :].astype(jnp.float32)
-        for mask in inner_masks:
+        own = pl.ds(pl.multiple_of(first + half * chunk, chunk), chunk)
+        total = paired[own, :].astype(jnp.float32)
+        for mask in chip_masks:
             total = total + part_in[half, mask].astype(jnp.float32)
         part[half] = total.astype(jnp.bfloat16)
         for mask in outer_masks:
@@ -202,7 +210,7 @@
             terms.append(plane_in[half, index].astype(jnp.float32))
         while len(terms) > 1:
             terms = [terms[i] + terms[i + 1] for i in range(0, len(terms), 2)]
-        rows = pl.ds(pl.multiple_of(half * width + mine * chunk, chunk), chunk)
+        rows = pl.ds(pl.multiple_of(core * width + first + half * chunk, chunk), chunk)
         gathered[rows, :] = terms[0].astype(jnp.bfloat16)
         for mask in inner_masks:
             copy = remote(
@@ -218,7 +226,7 @@
     for copy in gather_copies:
         copy.wait_recv()
 
-    for copy in row_copies + part_copies + grad_copies + plane_copies + gather_copies:
+    for copy in [pair_copy] + row_copies + part_copies + grad_copies + plane_copies + gather_copies:
         copy.wait_send()
 
 
@@ -271,10 +279,12 @@
             pltpu.VMEM((rows, width), bf16),
             pltpu.VMEM((rows, width), bf16),
             pltpu.VMEM((2, width, width), bf16),
+            pltpu.VMEM((width, width), bf16),
+            pltpu.VMEM((width, width), bf16),
             pltpu.VMEM((2, inner, chunk, width), bf16),
             pltpu.VMEM((2, chunk, width), bf16),
             pltpu.VMEM((2, outer, chunk, width), bf16),
-            sem((levels,)), sem((levels,)), sem((levels,)), sem((levels,)),
+            sem((1,)), sem((1,)), sem((levels,)), sem((levels,)), sem((levels,)), sem((levels,)),
             sem((2, inner)), sem((2, inner)), sem((2, outer)), sem((2, outer)), sem((2, inner)), sem((2, inner)),
         ],
         compiler_params=pltpu.CompilerParams(

time: 26.9 us -> 27.1 us (level)
  no operation moved by 1% of the time
where the time goes in v9:
time: 27.1 us; the launch traced here: 27 us
  Pallas kernels  26.3 us (97%)
  between operations  0.64 us (2%)
    pallas_call x1, Pallas kernels, per_device(): pl.pallas_call(functools.partial(kernel, inner, outer, levels, bnd), out_...  25.2 us
    pallas_call x1, Pallas kernels, per_device(): pl.pallas_call(finish, out_shape=(jax.ShapeDtypeStruct((nodes, width), bf...  1.15 us

profile of v9, /device:TPU:0, one launch (start us, length us, event | category | flops | bytes accessed | tf_op | source)
XLA Modules:
  0.0 27.0 jit_solution(12016803477970794834)
XLA Ops:
  0.6 25.2 %shard_map.94 = (bf16[512,256]{1,0:T(8,128)(2,1)S(1)}, bf16[512,256]{1,0:T(8,128)(2,1)S(1)}, bf16[512,256]{1,0:T(8,128)(2,1)S(1)}) custom-call(bf16[512,256]{1,0:T(8,128)(2,1)} %feat_hbm.1, bf16[256,256]{1,0:T(8,128)(2,1)} %w_self_hbm.1, bf16[256,256]{1,0:T(8,128)(2,1)} %w_neigh_hbm.1, s32[10,512]{1,0:T(8,128)} %bitcast.2, s32[512]{0:T(512)} %degree_hbm.1, ...), custom_call_target="tpu_custom_call" | custom-call | flops 1073741824 | bytes 3145728 | tf_op jit(solution)/shard_map/pallas_call | solution.py:263
  25.8 1.1 %shard_map.95 = (bf16[512,256]{1,0:T(8,128)(2,1)}, bf16[512,256]{1,0:T(8,128)(2,1)}, f32[512,256]{1,0:T(8,128)}) custom-call(bf16[512,256]{1,0:T(8,128)(2,1)S(1)} %get-tuple-element.6.hidden, bf16[512,256]{1,0:T(8,128)(2,1)S(1)} %get-tuple-element.7.node, bf16[512,256]{1,0:T(8,128)(2,1)S(1)} %get-tuple-element.8.gathered), custom_call_target="tpu_custom_call" | custom-call | flops 262144 | bytes 1048576 | tf_op jit(solution)/shard_map/pallas_call | solution.py:295

commit v10 on v7

--- a/solution.py
+++ b/solution.py
@@ -10,6 +10,7 @@
 epsilon = 1e-06
 INNER_BITS = 3
 BUILD_ROWS = 128
+FORWARD_NODES = 256
 
 
 def partner(me, mask):
@@ -40,7 +41,7 @@
     feat_hbm, w_self_hbm, w_neigh_hbm, slots_hbm, degree_hbm, boundary_hbm, up_hbm,
     hidden_ref, node_ref, gathered,
     feat_ref, w_self_ref, w_neigh_ref, slots_ref, degree_ref, boundary_ref, up_ref, fetch_sem,
-    feat_t, table, pick, out_rows, in_rows, out_grads, in_grads,
+    lefts, summed, pre_ref, hidden_t, pre_grad_ref, up_t, w_neigh_t, share_ref, table, pick, out_rows, in_rows, out_grads, in_grads,
     stack, part_in, part, plane_in,
     row_ss, row_rs, grad_ss, grad_rs, part_ss, part_rs, plane_ss, plane_rs, gather_ss, gather_rs,
 ):
@@ -80,13 +81,13 @@
 
     fetches[0].wait()
     fetches[1].wait()
-    feat_t[...] = jnp.transpose(feat_ref[...])
+    lefts[0] = jnp.transpose(feat_ref[...])
 
     row_id = lax.broadcasted_iota(jnp.int32, (nodes, bnd), 0)
     for level in range(levels):
         hot = (row_id == boundary_ref[level]).astype(jnp.float32).astype(jnp.bfloat16)
         pick[:, pl.ds(level * bnd, bnd)] = hot
-    picked = dot(feat_t[...], pick[...]).astype(jnp.bfloat16)
+    picked = dot(lefts[0], pick[...]).astype(jnp.bfloat16)
     for level in range(levels):
         out_rows[level] = picked[:, level * bnd : (level + 1) * bnd]
     pl.semaphore_wait(barrier, len(greeted))
@@ -118,41 +119,72 @@
 
     lax.fori_loop(0, total_rows // BUILD_ROWS, build, 0)
 
-    share = 1.0 / degree_row.astype(jnp.float32)
-    summed = dot(feat_t[...], table[:nodes, :])
+    share_ref[...] = 1.0 / degree_row.astype(jnp.float32)
     for fetch in fetches[4:]:
         fetch.wait()
-    pre_self = dot_rows(w_self_ref[...], feat_t[...])
-    w_neigh_t = jnp.transpose(w_neigh_ref[...])
-    up_t = jnp.transpose(up_ref[...])
-
+    w_neigh_t[...] = jnp.transpose(w_neigh_ref[...])
+    up_t[...] = jnp.transpose(up_ref[...])
+
+    def ahead(block, carry):
+        span = pl.ds(pl.multiple_of(block * FORWARD_NODES, FORWARD_NODES), FORWARD_NODES)
+        summed[:, span] = dot(lefts[0], table[:nodes, span])
+        pre_ref[:, span] = dot_rows(w_self_ref[...], lefts[0, :, span])
+        return carry
+
+    lax.fori_loop(0, nodes // FORWARD_NODES, ahead, 0)
+    for copy in row_copies:
+        copy.wait_recv()
+
+    def forward(block, carry):
+        span = pl.ds(pl.multiple_of(block * FORWARD_NODES, FORWARD_NODES), FORWARD_NODES)
+        rows_t = jnp.concatenate([in_rows[level] for level in range(levels)], axis=1)
+        agg = summed[:, span] + dot(rows_t, table[nodes:, span])
+        agg = (agg * share_ref[:, span]).astype(jnp.bfloat16)
+        lefts[1, :, span] = agg
+        pre_sum = pre_ref[:, span] + dot(w_neigh_t[...], agg)
+        sigmoid = jax.nn.sigmoid(pre_sum)
+        hidden_t[:, span] = (pre_sum * sigmoid).astype(jnp.bfloat16)
+        pre_grad_ref[:, span] = (
+            up_t[:, span].astype(jnp.float32) * sigmoid * (1.0 + pre_sum * (1.0 - sigmoid))
+        ).astype(jnp.bfloat16)
+        return carry
+
+    lax.fori_loop(0, nodes // FORWARD_NODES, forward, 0)
+
+    width = lefts.shape[1]
     inner_levels = inner.bit_length() - 1
-    for low, high in ((0, inner_levels), (inner_levels, levels)):
-        for level in range(low, high):
-            row_copies[level].wait_recv()
-        rows_t = jnp.concatenate([in_rows[level] for level in range(low, high)], axis=1)
-        summed = summed + dot(rows_t, table[nodes + low * bnd : nodes + high * bnd, :])
-    agg_t = (summed * share).astype(jnp.bfloat16)
-    pre_sum = pre_self + dot(w_neigh_t, agg_t)
-    sigmoid = jax.nn.sigmoid(pre_sum)
-    pre_grad = (
-        up_t.astype(jnp.float32) * sigmoid * (1.0 + pre_sum * (1.0 - sigmoid))
-    ).astype(jnp.bfloat16)
-
-    width = feat_t.shape[0]
-    part_copies = []
-    for half in range(2):
-        left_t = feat_t[...] if half == 0 else agg_t
-        stack[half] = dot_cols(left_t, pre_grad).astype(jnp.bfloat16)
-        for mask in inner_masks:
-            theirs = lax.rem(partner(me, mask), inner)
-            copy = remote(
-                stack.at[half, pl.ds(pl.multiple_of(theirs * chunk, chunk), chunk), :],
-                part_in.at[half, mask], part_ss.at[half, mask], part_rs.at[half, mask], mask,
-            )
-            copy.start()
-            part_copies.append(copy)
-
+
+    def part_copy(half, mask):
+        theirs = lax.rem(partner(me, mask), inner)
+        return remote(
+            stack.at[half, pl.ds(pl.multiple_of(theirs * chunk, chunk), chunk), :],
+            part_in.at[half, mask], part_ss.at[half, mask], part_rs.at[half, mask], mask,
+        )
+
+    def plane_copy(half, mask):
+        index = mask // inner
+        return remote(
+            part.at[half], plane_in.at[half, index],
+            plane_ss.at[half, index], plane_rs.at[half, index], mask,
+        )
+
+    def gather_copy(half, mask):
+        rows = pl.ds(pl.multiple_of(half * width + mine * chunk, chunk), chunk)
+        return remote(
+            gathered.at[rows, :], gathered.at[rows, :],
+            gather_ss.at[half, mask], gather_rs.at[half, mask], mask,
+        )
+
+    def send_parts(half, carry):
+        stack[half] = dot_cols(lefts[half], pre_grad_ref[...]).astype(jnp.bfloat16)
+        for mask in inner_masks:
+            part_copy(half, mask).start()
+        return carry
+
+    lax.fori_loop(0, 2, send_parts, 0)
+
+    pre_grad = pre_grad_ref[...]
+    share = share_ref[...]
     slot_share = (dot(w_neigh_ref[...], pre_grad) * share).astype(jnp.bfloat16)
     out_grads[...] = dot_cols(table[nodes:, :], slot_share).astype(jnp.bfloat16)
     grad_copies = []
@@ -167,36 +199,28 @@
 
     for level in reversed(range(inner_levels, levels)):
         return_grads(level)
-    hidden_ref[...] = jnp.transpose((pre_sum * sigmoid).astype(jnp.bfloat16))
+    hidden_ref[...] = jnp.transpose(hidden_t[...])
     local = jnp.transpose(dot(w_self_ref[...], pre_grad)) + dot_cols(table[:nodes, :], slot_share)
 
     own = pl.ds(pl.multiple_of(mine * chunk, chunk), chunk)
-    per_half = len(inner_masks)
-    plane_copies = []
-    for half in range(2):
-        for copy in part_copies[half * per_half : (half + 1) * per_half]:
-            copy.wait_recv()
+    def send_planes(half, carry):
+        for mask in inner_masks:
+            part_copy(half, mask).wait_recv()
         total = stack[half, own, :].astype(jnp.float32)
         for mask in inner_masks:
             total = total + part_in[half, mask].astype(jnp.float32)
         part[half] = total.astype(jnp.bfloat16)
         for mask in outer_masks:
-            index = mask // inner
-            copy = remote(
-                part.at[half], plane_in.at[half, index],
-                plane_ss.at[half, index], plane_rs.at[half, index], mask,
-            )
-            copy.start()
-            plane_copies.append(copy)
-
+            plane_copy(half, mask).start()
+        return carry
+
+    lax.fori_loop(0, 2, send_planes, 0)
     for level in reversed(range(inner_levels)):
         return_grads(level)
 
-    per_outer = len(outer_masks)
-    gather_copies = []
-    for half in range(2):
-        for copy in plane_copies[half * per_outer : (half + 1) * per_outer]:
-            copy.wait_recv()
+    def send_gathers(half, carry):
+        for mask in outer_masks:
+            plane_copy(half, mask).wait_recv()
         terms = [part[half].astype(jnp.float32)]
         for index in range(1, outer):
             terms.append(plane_in[half, index].astype(jnp.float32))
@@ -205,20 +229,25 @@
         rows = pl.ds(pl.multiple_of(half * width + mine * chunk, chunk), chunk)
         gathered[rows, :] = terms[0].astype(jnp.bfloat16)
         for mask in inner_masks:
-            copy = remote(
-                gathered.at[rows, :], gathered.at[rows, :],
-                gather_ss.at[half, mask], gather_rs.at[half, mask], mask,
-            )
-            copy.start()
-            gather_copies.append(copy)
+            gather_copy(half, mask).start()
+        return carry
+
+    lax.fori_loop(0, 2, send_gathers, 0)
 
     for copy in grad_copies:
         copy.wait_recv()
     node_ref[...] = (local + dot(pick[...], in_grads[...])).astype(jnp.bfloat16)
-    for copy in gather_copies:
-        copy.wait_recv()
-
-    for copy in row_copies + part_copies + grad_copies + plane_copies + gather_copies:
+
+    def settle(half, carry):
+        for mask in inner_masks:
+            part_copy(half, mask).wait_send()
+            gather_copy(half, mask).wait()
+        for mask in outer_masks:
+            plane_copy(half, mask).wait_send()
+        return carry
+
+    lax.fori_loop(0, 2, settle, 0)
+    for copy in row_copies + grad_copies:
         copy.wait_send()
 
 
@@ -263,7 +292,14 @@
         out_specs=(vmem, vmem, vmem),
         scratch_shapes=[pltpu.VMEM(arg.shape, arg.dtype) for arg in args] + [
             sem((7,)),
+            pltpu.VMEM((2, width, nodes), bf16),
+            pltpu.VMEM((width, nodes), jnp.float32),
+            pltpu.VMEM((width, nodes), jnp.float32),
             pltpu.VMEM((width, nodes), bf16),
+            pltpu.VMEM((width, nodes), bf16),
+            pltpu.VMEM((width, nodes), bf16),
+            pltpu.VMEM((width, width), bf16),
+            pltpu.VMEM((1, nodes), jnp.float32),
             pltpu.VMEM((nodes + rows, nodes), bf16),
             pltpu.VMEM((nodes, rows), bf16),
             pltpu.VMEM((levels, width, bnd), bf16),

time: 26.9 us -> 27.3 us (1.015)
  Pallas kernels: 26.1 us -> 26.5 us
    pallas_call x1, Pallas kernels: 25 us -> 25.4 us  [per_device(): pl.pallas_call(functools.partial(kernel, inner, outer, levels, bnd), out_...]
where the time goes in v10:
time: 27.3 us; the launch traced here: 27.2 us
  Pallas kernels  26.5 us (97%)
  between operations  0.64 us (2%)
    pallas_call x1, Pallas kernels, per_device(): pl.pallas_call(functools.partial(kernel, inner, outer, levels, bnd), out_...  25.4 us
    pallas_call x1, Pallas kernels, per_device(): pl.pallas_call(finish, out_shape=(jax.ShapeDtypeStruct((nodes, width), bf...  1.15 us

profile of v10, /device:TPU:0, one launch (start us, length us, event | category | flops | bytes accessed | tf_op | source)
XLA Modules:
  0.0 27.2 jit_solution(1640483698796116041)
XLA Ops:
  0.6 25.4 %shard_map.94 = (bf16[512,256]{1,0:T(8,128)(2,1)S(1)}, bf16[512,256]{1,0:T(8,128)(2,1)S(1)}, bf16[512,256]{1,0:T(8,128)(2,1)S(1)}) custom-call(bf16[512,256]{1,0:T(8,128)(2,1)} %feat_hbm.1, bf16[256,256]{1,0:T(8,128)(2,1)} %w_self_hbm.1, bf16[256,256]{1,0:T(8,128)(2,1)} %w_neigh_hbm.1, s32[10,512]{1,0:T(8,128)} %bitcast.2, s32[512]{0:T(512)} %degree_hbm.1, ...), custom_call_target="tpu_custom_call" | custom-call | flops 1073741824 | bytes 3145728 | tf_op jit(solution)/shard_map/pallas_call | solution.py:284
  26.0 1.1 %shard_map.95 = (bf16[512,256]{1,0:T(8,128)(2,1)}, bf16[512,256]{1,0:T(8,128)(2,1)}, f32[512,256]{1,0:T(8,128)}) custom-call(bf16[512,256]{1,0:T(8,128)(2,1)S(1)} %get-tuple-element.6.hidden, bf16[512,256]{1,0:T(8,128)(2,1)S(1)} %get-tuple-element.7.node, bf16[512,256]{1,0:T(8,128)(2,1)S(1)} %get-tuple-element.8.gathered), custom_call_target="tpu_custom_call" | custom-call | flops 262144 | bytes 1048576 | tf_op jit(solution)/shard_map/pallas_call | solution.py:321
